TPU v7x, 32 devices: a whole 2x2x4 slice. The times are simulated.
32 devices in a mesh: groups: 2 (over x), lat: 16 (over z, y, core).
Axes of the slice: x: 2, y: 2, z: 4, core: 2. Of those that a mesh axis runs over, the one named last changes fastest.
Arguments:
- tangent: float32 [128, 128, 1024], P(('groups', 'lat')), parts along dimension 0, may hold values from -6 to 6
- wind_code: int32 [4, 128, 128], P(None, ('groups', 'lat')), parts along dimension 1, may hold values from 0 to 14
- courant: float32 [1024], replicated, may hold values from 0.2 to 0.8
- obs_index: int32 [32, 480], P(('groups', 'lat')), parts along dimension 0, may hold values from 0 to 511, as said below
- obs_count: int32 [32], P(('groups', 'lat')), parts along dimension 0, may hold values from 96 to 480, as said below
- obs_quality: bfloat16 [32, 480], P(('groups', 'lat')), parts along dimension 0, may hold values from 0.29882812 to 3
- background: bfloat16 [32, 480, 1024], P(('groups', 'lat')), parts along dimension 0, may hold values from -6 to 6
- w_first: bfloat16 [1024, 1024], replicated, may hold values from -0.1875 to 0.1875
- w_second: bfloat16 [1024, 1024], replicated, may hold values from -0.1875 to 0.1875
- w_third: bfloat16 [1024, 1024], replicated, may hold values from -0.1875 to 0.1875
- chan_weight: float32 [1024], replicated, may hold values from 0.3 to 3
Outputs:
- adjoint_field: float32 [128, 128, 1024], P(('groups', 'lat')), parts along dimension 0
There are 2 independent parts, one for each index of `groups`. A program takes and returns all parts, laid end to end along the dimension named above; an argument that names none is the same for every part. Nothing has to cross between parts.
Inputs may be any that keep to these rules, and one draw needn't show every extreme that they name: `obs_count`: the counts of all tiles sum to 192 times the number of tiles, and some tile has 480. `obs_index`: the 480 entries of one tile are distinct; the first obs_count of them are the observed columns.
All inputs are finite; a program needn't handle non-finite values.
Results may differ from a plain program's by a relative error of at most 0.0055.
Values may be sent and summed in bfloat16 or wider, within the bound.
No kernel may reach another device: no remote copies, remote signals or barrier semaphores. Data moves between devices by JAX's collectives and lax.ppermute only.
A program may use at most 64 MiB of HBM per device.

v0:
```python
import functools

import jax
import jax.numpy as jnp
from jax import lax
from jax.experimental import pallas as pl
from jax.experimental.pallas import tpu as pltpu
from jax.sharding import PartitionSpec as P

F32 = jnp.float32
BF16 = jnp.bfloat16
LANE = 256
ANY = pl.BlockSpec(memory_space=pl.ANY)
VMEM = pl.BlockSpec(memory_space=pltpu.VMEM)
SMEM = pl.BlockSpec(memory_space=pltpu.SMEM)
VMEM_LIMIT = 56 * 1024 * 1024


def dot_t(left, right):
    return lax.dot_general(left, right, (((1,), (1,)), ((), ())), preferred_element_type=F32)


def dot(left, right):
    return jnp.dot(left, right, preferred_element_type=F32)


def store_sources(table, slot, codes, mirrored, sign, lon, rows):
    code = codes.astype(F32) - 1.0
    lat_q = jnp.where(code >= 5.0, 1.0, 0.0) + jnp.where(code >= 10.0, 1.0, 0.0)
    lon_step = code - 5.0 * lat_q - 2.0
    col = lax.broadcasted_iota(jnp.int32, code.shape, 1).astype(F32) - lon_step
    col = jnp.where(col < 0.0, col + lon, jnp.where(col >= lon, col - lon, col))
    stored = lax.broadcasted_iota(jnp.int32, code.shape, 0) & (rows - 1)
    row = (rows - 1 - stored) if mirrored else stored
    row = (row + slot * rows).astype(F32)
    src = (row - sign * (lat_q - 1.0)) * lon + col
    table[slot * code.shape[0] : (slot + 1) * code.shape[0], :] = jnp.where(code < 0.0, -65536.0, src)


def table_row(step, ext, rows):
    slot, at = ext // rows, ext % rows
    return slot * rows * rows + step * rows + (at if slot == 1 else rows - 1 - at)


def pull_matrix(out, turned, step, ext, lon, rows):
    span = 4 * lon
    lanes = lax.broadcasted_iota(jnp.int32, (lon, span), 1).astype(F32) + float((ext - 1) * lon)
    for half in range(2):
        k = table_row(step, ext + half, rows)
        column = turned[:, k : k + 1]
        out[half * lon : (half + 1) * lon, :] = jnp.where(column == lanes, 1.0, 0.0).astype(BF16)


def push_matrix(out, table, step, ext, lon, rows):
    dest = lax.broadcasted_iota(jnp.int32, (2 * lon, lon), 0).astype(F32) + float(ext * lon)
    for part in range(4):
        k = table_row(step, ext - 1 + part, rows)
        line = table[k : k + 1, :]
        out[:, part * lon : (part + 1) * lon] = jnp.where(line == dest, 1.0, 0.0).astype(BF16)


def pack_kernel(flip, tangent, codes, out, buf, sem):
    rows, lon = tangent.shape[0], tangent.shape[1]
    copies = []
    for j in range(rows):
        at = jnp.where(flip[0] == 1, rows - 1 - j, j)
        copies.append(pltpu.make_async_copy(tangent.at[at], buf.at[j], sem.at[j]))
        copies[-1].start()
    pad = jnp.zeros((codes.shape[0], out.shape[1] - lon), BF16)
    out[rows * lon :, :] = jnp.concatenate([codes[...].astype(F32).astype(BF16), pad], axis=1)
    for j in range(rows):
        copies[j].wait()
        out[j * lon : (j + 1) * lon, :] = buf[j].astype(BF16)


def near_steps(mats, start_b, start_f, c_ref, outs, mid_b, mid_f, lon, cs):
    c = c_ref[0:1, cs]
    blocks = ((5, 7, 9), (6, 8), (7,))
    read_b, read_f, first = start_b, start_f, 4
    k = 0
    for step, exts in enumerate(blocks):
        for ext in exts:
            at = (ext - 1 - first) * lon
            pulled = dot(mats[k], read_b(at, 4 * lon))
            value = (1.0 - c) * read_f(at + lon, 2 * lon) + c * pulled
            k += 1
            if ext == exts[0]:
                outs[step][:, cs] = value
            if step < 2:
                to = (ext - exts[0]) * lon
                mid_f[step, to : to + 2 * lon, :] = value
                mid_b[step, to : to + 2 * lon, :] = value.astype(BF16)
        first = exts[0]
        read_b = functools.partial(lambda s, a, n: mid_b[s, a : a + n, :], step)
        read_f = functools.partial(lambda s, a, n: mid_f[s, a : a + n, :], step)


def far_steps(mats, start_b, start_f, c_ref, kept, mid_b, mid_f, lon, cs):
    c = c_ref[0:1, cs]
    k = 0
    done = []
    for step in range(4):
        for half in range(2):
            at = 2 * half * lon
            if step == 0:
                window, own = start_b(at, 4 * lon), start_f(at + lon, 2 * lon)
            else:
                window = mid_b[step - 1, at : at + 4 * lon, :]
                own = mid_f[step - 1, at + lon : at + 3 * lon, :]
            value = (1.0 - c) * own + c * dot(mats[k], window)
            k += 1
            if step < 3:
                mid_f[step, at : at + 2 * lon, :] = value
                mid_b[step, at : at + 2 * lon, :] = value.astype(BF16)
            else:
                done.append(value)
        if step < 3:
            carried = kept[step][:, cs]
            mid_f[step, 4 * lon :, :] = carried
            mid_b[step, 4 * lon :, :] = carried.astype(BF16)
    return done


def near_kernel(
    flip, tangent, own, near, courant, background, w_first, w_second,
    slope_one, slope_two, kept_a, kept_b, kept_c,
    table, mats, cells_f, cells_b, mid_b, mid_f, back, w_one, w_two, hidden, s_one, s_two, sem,
):
    rows, lon = tangent.shape[0], tangent.shape[1]
    levels = tangent.shape[2]
    loads = [
        pltpu.make_async_copy(background, back, sem.at[0]),
        pltpu.make_async_copy(w_first, w_one, sem.at[1]),
        pltpu.make_async_copy(w_second, w_two, sem.at[2]),
    ]
    for copy in loads:
        copy.start()
    cell_copies = []
    for j in range(rows):
        at = jnp.where(flip[0] == 1, rows - 1 - j, j)
        cell_copies.append(pltpu.make_async_copy(tangent.at[at], cells_f.at[j], sem.at[5 + j]))
        cell_copies[-1].start()

    sign = jnp.where(flip[0] == 1, -1.0, 1.0)
    cells = rows * lon
    table[...] = jnp.zeros_like(table)
    store_sources(table, 1, own[cells:, 0:lon], False, sign, lon, rows)
    store_sources(table, 2, near[cells:, 0:lon], True, sign, lon, rows)
    turned = table[...].T
    k = 0
    for step, exts in enumerate(((5, 7, 9), (6, 8), (7,))):
        for ext in exts:
            pull_matrix(mats.at[k], turned, step, ext, lon, rows)
            k += 1
    cells_b[0:cells, :] = own[0:cells, :]
    for j in range(rows):
        cells_b[(rows + j) * lon : (rows + j + 1) * lon, :] = near[(rows - 1 - j) * lon : (rows - j) * lon, :]
    for copy in cell_copies:
        copy.wait()

    @pl.loop(0, levels // LANE)
    def _(i):
        cs = pl.ds(pl.multiple_of(i * LANE, LANE), LANE)

        def start_f(at, size):
            pieces = []
            for row in range(at // lon, (at + size) // lon):
                if row < rows:
                    pieces.append(cells_f[row, :, cs])
                else:
                    pieces.append(cells_b[row * lon : (row + 1) * lon, cs].astype(F32))
            return jnp.concatenate(pieces, axis=0)

        near_steps(
            mats, lambda at, size: cells_b[at : at + size, cs], start_f, courant,
            (kept_a, kept_b, kept_c), mid_b, mid_f, lon, cs,
        )

    loads[0].wait()
    loads[1].wait()

    @pl.loop(0, levels // LANE)
    def _(i):
        cs = pl.ds(pl.multiple_of(i * LANE, LANE), LANE)
        first_tanh = jnp.tanh(dot(back[...], w_one[:, cs]))
        hidden[:, cs] = first_tanh.astype(BF16)
        s_one[:, cs] = 1.0 - first_tanh * first_tanh

    keep_one = pltpu.make_async_copy(s_one, slope_one, sem.at[3])
    keep_one.start()
    loads[2].wait()

    @pl.loop(0, levels // LANE)
    def _(i):
        cs = pl.ds(pl.multiple_of(i * LANE, LANE), LANE)
        second_tanh = jnp.tanh(dot(hidden[...], w_two[:, cs]))
        s_two[:, cs] = 1.0 - second_tanh * second_tanh

    keep_two = pltpu.make_async_copy(s_two, slope_two, sem.at[4])
    keep_two.start()
    keep_one.wait()
    keep_two.wait()


def observe_kernel(
    flip, tangent, own, near, far, courant, slope_one, slope_two, kept_a, kept_b, kept_c,
    w_first, w_second, w_third, where_col, where_row, quality, chan_weight,
    out,
    table, mats, row_f, cells_b, mid_b, mid_f, last_b, w_one, w_two, w_three, s_one, s_two,
    pick, place, one_b, two_b, sem,
):
    rows, lon = tangent.shape[0], tangent.shape[1]
    levels = tangent.shape[2]
    loads = [
        pltpu.make_async_copy(w_first, w_one, sem.at[0]),
        pltpu.make_async_copy(slope_one, s_one, sem.at[1]),
        pltpu.make_async_copy(w_second, w_two, sem.at[2]),
        pltpu.make_async_copy(slope_two, s_two, sem.at[3]),
        pltpu.make_async_copy(w_third, w_three, sem.at[4]),
    ]
    at0 = jnp.where(flip[0] == 1, rows - 1, 0)
    row_copy = pltpu.make_async_copy(tangent.at[at0], row_f, sem.at[5])
    row_copy.start()
    for copy in loads:
        copy.start()

    sign = jnp.where(flip[0] == 1, -1.0, 1.0)
    cells = rows * lon
    table[...] = jnp.zeros_like(table)
    store_sources(table, 0, far[cells:, 0:lon], True, sign, lon, rows)
    store_sources(table, 1, own[cells:, 0:lon], False, sign, lon, rows)
    turned = table[...].T
    for step in range(4):
        for half in range(2):
            pull_matrix(mats.at[2 * step + half], turned, step, step + 1 + 2 * half, lon, rows)
    for j in range(rows):
        cells_b[j * lon : (j + 1) * lon, :] = far[(rows - 1 - j) * lon : (rows - j) * lon, :]
    cells_b[cells:, :] = own[0 : 2 * lon, :]
    slots = where_col.shape[0]
    pick[...] = jnp.where(
        where_col[...] == lax.broadcasted_iota(jnp.int32, (slots, cells), 1), 1.0, 0.0
    ).astype(BF16)
    place[...] = jnp.where(
        where_row[...] == lax.broadcasted_iota(jnp.int32, (cells, slots), 0), 1.0, 0.0
    ).astype(BF16)
    row_copy.wait()

    @pl.loop(0, levels // LANE)
    def _(i):
        cs = pl.ds(pl.multiple_of(i * LANE, LANE), LANE)

        def start_f(at, size):
            pieces = []
            for row in range(at // lon, (at + size) // lon):
                if row == rows:
                    pieces.append(row_f[:, cs])
                else:
                    pieces.append(cells_b[row * lon : (row + 1) * lon, cs].astype(F32))
            return jnp.concatenate(pieces, axis=0)

        done = far_steps(
            mats, lambda at, size: cells_b[at : at + size, cs], start_f, courant,
            (kept_a, kept_b, kept_c), mid_b, mid_f, lon, cs,
        )
        for half in range(2):
            last_b[2 * half * lon : 2 * (half + 1) * lon, :] = done[half].astype(BF16)
        one_b[:, cs] = dot(pick[...], last_b[...]).astype(BF16)

    def layer(body):
        @pl.loop(0, levels // LANE)
        def _(i):
            body(pl.ds(pl.multiple_of(i * LANE, LANE), LANE))

    loads[0].wait()
    loads[1].wait()

    def tangent_one(cs):
        two_b[:, cs] = (s_one[:, cs] * dot(one_b[...], w_one[:, cs])).astype(BF16)

    layer(tangent_one)
    loads[2].wait()
    loads[3].wait()

    def tangent_two(cs):
        one_b[:, cs] = (s_two[:, cs] * dot(two_b[...], w_two[:, cs])).astype(BF16)

    layer(tangent_two)
    loads[4].wait()

    def weighted(cs):
        scale = quality[...] * chan_weight[0:1, cs]
        two_b[:, cs] = (scale * dot(one_b[...], w_three[:, cs])).astype(BF16)

    layer(weighted)

    def adjoint_two(cs):
        one_b[:, cs] = (s_two[:, cs] * dot_t(two_b[...], w_three[cs, :])).astype(BF16)

    layer(adjoint_two)

    def adjoint_one(cs):
        two_b[:, cs] = (s_one[:, cs] * dot_t(one_b[...], w_two[cs, :])).astype(BF16)

    layer(adjoint_one)

    def adjoint_cells(cs):
        column = dot_t(two_b[...], w_one[cs, :]).astype(BF16)
        out[:, cs] = dot(place[...], column).astype(BF16)

    layer(adjoint_cells)


def near_adjoint_kernel(
    flip, cells_own, cells_near, own, near, courant,
    kept_a, kept_b, kept_c,
    table, mats, cells_b, mid_b, mid_f,
):
    levels = cells_own.shape[1]
    rows, lon = 4, table.shape[1]
    cells = rows * lon
    sign = jnp.where(flip[0] == 1, -1.0, 1.0)
    store_sources(table, 1, own[cells:, 0:lon], False, sign, lon, rows)
    store_sources(table, 2, near[cells:, 0:lon], True, sign, lon, rows)
    k = 0
    for order, exts in enumerate(((5, 7, 9), (6, 8), (7,))):
        for ext in exts:
            push_matrix(mats.at[k], table, 3 - order, ext, lon, rows)
            k += 1
    cells_b[0:cells, :] = cells_own[...]
    for j in range(rows):
        cells_b[(rows + j) * lon : (rows + j + 1) * lon, :] = cells_near[
            (rows - 1 - j) * lon : (rows - j) * lon, :
        ]

    @pl.loop(0, levels // LANE)
    def _(i):
        cs = pl.ds(pl.multiple_of(i * LANE, LANE), LANE)
        near_steps(
            mats, lambda at, size: cells_b[at : at + size, cs],
            lambda at, size: cells_b[at : at + size, cs].astype(F32), courant,
            (kept_a, kept_b, kept_c), mid_b, mid_f, lon, cs,
        )


def far_adjoint_kernel(
    flip, cells_own, cells_far, own, far, courant, kept_a, kept_b, kept_c,
    out,
    table, mats, cells_b, mid_b, mid_f, result, sem,
):
    levels = cells_own.shape[1]
    rows, lon = 4, table.shape[1]
    cells = rows * lon
    sign = jnp.where(flip[0] == 1, -1.0, 1.0)
    store_sources(table, 0, far[cells:, 0:lon], True, sign, lon, rows)
    store_sources(table, 1, own[cells:, 0:lon], False, sign, lon, rows)
    for order in range(4):
        for half in range(2):
            push_matrix(mats.at[2 * order + half], table, 3 - order, order + 1 + 2 * half, lon, rows)
    for j in range(rows):
        cells_b[j * lon : (j + 1) * lon, :] = cells_far[(rows - 1 - j) * lon : (rows - j) * lon, :]
    cells_b[cells:, :] = cells_own[0 : 2 * lon, :]

    @pl.loop(0, levels // LANE)
    def _(i):
        cs = pl.ds(pl.multiple_of(i * LANE, LANE), LANE)
        done = far_steps(
            mats, lambda at, size: cells_b[at : at + size, cs],
            lambda at, size: cells_b[at : at + size, cs].astype(F32), courant,
            (kept_a, kept_b, kept_c), mid_b, mid_f, lon, cs,
        )
        for half in range(2):
            for part in range(2):
                result[2 * half + part, :, cs] = done[half][part * lon : (part + 1) * lon, :]

    copies = []
    for j in range(rows):
        at = jnp.where(flip[0] == 1, rows - 1 - j, j)
        copies.append(pltpu.make_async_copy(result.at[j], out.at[at], sem.at[j]))
        copies[-1].start()
    for copy in copies:
        copy.wait()


def params():
    return pltpu.CompilerParams(vmem_limit_bytes=VMEM_LIMIT)


def local(
    tangent,
    wind_code,
    courant,
    obs_index,
    obs_count,
    obs_quality,
    background,
    w_first,
    w_second,
    w_third,
    chan_weight,
):
    rows, lon, levels = tangent.shape
    steps = wind_code.shape[0]
    cells = rows * lon
    slots = obs_index.shape[1]
    hidden_size = w_first.shape[1]
    count = lax.axis_size("lat")
    here = lax.axis_index("lat")
    odd = (here % 2).astype(jnp.int32)
    flip = odd.reshape(1)
    pairs = [(i, i ^ 1) for i in range(count)]
    links = [(i, i + 1) for i in range(1, count - 1, 2)]
    links = links + [(b, a) for a, b in links]

    codes = jnp.where(odd == 1, wind_code[:, ::-1], wind_code) + 1
    codes = codes.reshape(steps * rows, lon)
    own = pl.pallas_call(
        pack_kernel,
        out_shape=jax.ShapeDtypeStruct((cells + steps * rows, levels), BF16),
        in_specs=[SMEM, ANY, VMEM],
        out_specs=VMEM,
        scratch_shapes=[pltpu.VMEM((rows, lon, levels), F32), pltpu.SemaphoreType.DMA((rows,))],
        compiler_params=params(),
        name="pack",
    )(flip, tangent, codes)

    near = lax.ppermute(own, "lat", pairs)
    far = lax.ppermute(own, "lat", links)

    c_row = courant.reshape(1, levels)
    slot_ids = jnp.arange(slots, dtype=jnp.int32)
    observed = slot_ids < obs_count[0]
    where_at = obs_index[0]
    where_at = jnp.where(odd == 1, where_at + (rows - 1 - 2 * (where_at // lon)) * lon, where_at)
    where_at = jnp.where(observed, where_at, -1)
    quality = jnp.where(observed, obs_quality[0].astype(F32), 0.0)

    kept_shape = [jax.ShapeDtypeStruct((2 * lon, levels), F32)] * 3
    slope_shape = jax.ShapeDtypeStruct((slots, hidden_size), F32)
    slope_one, slope_two, kept_a, kept_b, kept_c = pl.pallas_call(
        near_kernel,
        out_shape=[slope_shape, slope_shape] + kept_shape,
        in_specs=[SMEM, ANY, VMEM, VMEM, VMEM, ANY, ANY, ANY],
        out_specs=[ANY, ANY, VMEM, VMEM, VMEM],
        scratch_shapes=[
            pltpu.VMEM((lon, lon), F32),
            pltpu.VMEM((6, 2 * lon, 4 * lon), BF16),
            pltpu.VMEM((rows, lon, levels), F32),
            pltpu.VMEM((2 * cells, levels), BF16),
            pltpu.VMEM((2, 6 * lon, LANE), BF16),
            pltpu.VMEM((2, 6 * lon, LANE), F32),
            pltpu.VMEM((slots, levels), BF16),
            pltpu.VMEM(w_first.shape, BF16),
            pltpu.VMEM(w_second.shape, BF16),
            pltpu.VMEM((slots, hidden_size), BF16),
            pltpu.VMEM((slots, hidden_size), F32),
            pltpu.VMEM((slots, hidden_size), F32),
            pltpu.SemaphoreType.DMA((5 + rows,)),
        ],
        compiler_params=params(),
        cost_estimate=pl.CostEstimate(flops=4_000_000_000, bytes_accessed=16_000_000, transcendentals=1_000_000),
        name="near",
    )(flip, tangent, own, near, c_row, background[0], w_first, w_second)

    cells_own = pl.pallas_call(
        observe_kernel,
        out_shape=jax.ShapeDtypeStruct((cells, levels), BF16),
        in_specs=[SMEM, ANY, VMEM, VMEM, VMEM, VMEM, ANY, ANY, VMEM, VMEM, VMEM, ANY, ANY, ANY]
        + [VMEM] * 4,
        out_specs=VMEM,
        scratch_shapes=[
            pltpu.VMEM((lon, lon), F32),
            pltpu.VMEM((8, 2 * lon, 4 * lon), BF16),
            pltpu.VMEM((lon, levels), F32),
            pltpu.VMEM((6 * lon, levels), BF16),
            pltpu.VMEM((3, 6 * lon, LANE), BF16),
            pltpu.VMEM((3, 6 * lon, LANE), F32),
            pltpu.VMEM((cells, LANE), BF16),
            pltpu.VMEM(w_first.shape, BF16),
            pltpu.VMEM(w_second.shape, BF16),
            pltpu.VMEM(w_third.shape, BF16),
            pltpu.VMEM((slots, hidden_size), F32),
            pltpu.VMEM((slots, hidden_size), F32),
            pltpu.VMEM((slots, cells), BF16),
            pltpu.VMEM((cells, slots), BF16),
            pltpu.VMEM((slots, levels), BF16),
            pltpu.VMEM((slots, levels), BF16),
            pltpu.SemaphoreType.DMA((6,)),
        ],
        compiler_params=params(),
        name="observe",
    )(
        flip, tangent, own, near, far, c_row, slope_one, slope_two, kept_a, kept_b, kept_c,
        w_first, w_second, w_third, where_at.reshape(slots, 1), where_at.reshape(1, slots),
        quality.reshape(slots, 1), chan_weight.reshape(1, -1),
    )

    cells_near = lax.ppermute(cells_own, "lat", pairs)
    cells_far = lax.ppermute(cells_own, "lat", links)

    kept_a, kept_b, kept_c = pl.pallas_call(
        near_adjoint_kernel,
        out_shape=kept_shape,
        in_specs=[SMEM] + [VMEM] * 5,
        out_specs=[VMEM] * 3,
        scratch_shapes=[
            pltpu.VMEM((lon, lon), F32),
            pltpu.VMEM((6, 2 * lon, 4 * lon), BF16),
            pltpu.VMEM((2 * cells, levels), BF16),
            pltpu.VMEM((2, 6 * lon, LANE), BF16),
            pltpu.VMEM((2, 6 * lon, LANE), F32),
        ],
        compiler_params=params(),
        cost_estimate=pl.CostEstimate(flops=2_000_000_000, bytes_accessed=8_000_000, transcendentals=0),
        name="near_adjoint",
    )(flip, cells_own, cells_near, own, near, c_row)

    return pl.pallas_call(
        far_adjoint_kernel,
        out_shape=jax.ShapeDtypeStruct((rows, lon, levels), F32),
        in_specs=[SMEM] + [VMEM] * 8,
        out_specs=ANY,
        scratch_shapes=[
            pltpu.VMEM((lon, lon), F32),
            pltpu.VMEM((8, 2 * lon, 4 * lon), BF16),
            pltpu.VMEM((6 * lon, levels), BF16),
            pltpu.VMEM((3, 6 * lon, LANE), BF16),
            pltpu.VMEM((3, 6 * lon, LANE), F32),
            pltpu.VMEM((rows, lon, levels), F32),
            pltpu.SemaphoreType.DMA((rows,)),
        ],
        compiler_params=params(),
        name="far_adjoint",
    )(flip, cells_own, cells_far, own, far, c_row, kept_a, kept_b, kept_c)


def solution(mesh):
    placed = (
        P(("groups", "lat"), None, None),
        P(None, ("groups", "lat"), None),
        P(),
        P(("groups", "lat"), None),
        P(("groups", "lat")),
        P(("groups", "lat"), None),
        P(("groups", "lat"), None, None),
        P(),
        P(),
        P(),
        P(),
    )
    return jax.shard_map(
        local,
        mesh=mesh,
        in_specs=placed,
        out_specs=P(("groups", "lat"), None, None),
        check_vma=False,
    )
```

profile of v0, /device:TPU:25, one launch (start us, length us, event | category | flops | bytes accessed | tf_op | source)
XLA Modules:
  0.0 97.5 jit_solution(9634822239056325645)
XLA Ops:
  0.0 0.0 copy-start.4
  0.0 0.0 copy-start.3
  0.0 0.7 rev.3
  0.8 0.6 select_add_fusion
  1.4 3.3 %pack.1.own = bf16[528,1024]{1,0:T(8,128)(2,1)} custom-call(s32[1]{0:T(128)} %bitcast.flip, f32[4,128,1024]{2,1,0:T(8,128)} %tangent.5, s32[16,128]{1,0:T(8,128)} %bitcast.13), custom_call_target="tpu_custom_call" | custom-call | tf_op jit(solution)/shard_map/pack/pallas_call | solution.py:416
  4.6 1.4 %collective-permute-start = (bf16[528,1024]{1,0:T(8,128)(2,1)}, bf16[528,1024]{1,0:T(8,128)(2,1)S(1)}, u32[]{:S(2)}, u32[]{:S(2)}) collective-permute-start(bf16[528,1024]{1,0:T(8,128)(2,1)} %pack.1.own), channel_id=1, source_target_pairs={{0,1},{1,0},{2,3},{3,2},{4,5},{5,4},{6,7},{7,6},{8,9},{9,8},{10,11... | collective-permute-start | bytes 3244040 | tf_op jit(solution)/shard_map/ppermute | solution.py:426
  6.1 3.0 %collective-permute-start.1 = (bf16[528,1024]{1,0:T(8,128)(2,1)}, bf16[528,1024]{1,0:T(8,128)(2,1)S(1)}, u32[]{:S(2)}, u32[]{:S(2)}) collective-permute-start(bf16[528,1024]{1,0:T(8,128)(2,1)} %pack.1.own), channel_id=1, source_target_pairs={{1,2},{3,4},{5,6},{7,8},{9,10},{11,12},{13,14},{2,1},{4,3},{6,5},{... | collective-permute-start | bytes 3244040 | tf_op jit(solution)/shard_map/ppermute | solution.py:427
  9.1 0.0 copy-done.4
  9.8 0.1 copy.18
  9.9 0.0 copy-done.3
  10.0 0.1 copy.16
  10.1 0.6 compare_select_fusion.where_row
  10.6 0.7 fusion.5.quality
  11.4 0.9 fusion.4.where_col
  12.3 0.0 collective-permute-done.near
  12.3 0.0 copy-start.1
  12.3 1.0 %copy-done.1 = bf16[528,1024]{1,0:T(8,128)(2,1)} copy-done((bf16[528,1024]{1,0:T(8,128)(2,1)}, bf16[528,1024]{1,0:T(8,128)(2,1)S(1)}, u32[]{:S(2)}) %copy-start.1) | copy-done | bytes 1081368
  13.3 14.6 %near.1 = (f32[480,1024]{1,0:T(8,128)}, f32[480,1024]{1,0:T(8,128)}, f32[256,1024]{1,0:T(8,128)}, f32[256,1024]{1,0:T(8,128)}, f32[256,1024]{1,0:T(8,128)}) custom-call(s32[1]{0:T(128)} %bitcast.flip, f32[4,128,1024]{2,1,0:T(8,128)} %tangent.5, bf16[528,1024]{1,0:T(8,128)(2,1)} %pack.1.own, bf16[528,1024]{1,0:T(8,128)(2,1)} %copy-done.1, ...), custom_call_target="tpu_custom_call" | custom-call | flops 4000000000 | bytes 16000000 | tf_op jit(solution)/shard_map/near/pallas_call | solution.py:439
  27.9 6.5 %collective-permute-done.1.far = bf16[528,1024]{1,0:T(8,128)(2,1)S(1)} collective-permute-done((bf16[528,1024]{1,0:T(8,128)(2,1)}, bf16[528,1024]{1,0:T(8,128)(2,1)S(1)}, u32[]{:S(2)}, u32[]{:S(2)}) %collective-permute-start.1) | collective-permute-done | bytes 1081376 | tf_op jit(solution)/shard_map/ppermute | solution.py:427
  34.3 0.0 copy-start
  34.3 1.0 copy-done
  35.3 23.6 %observe.1.cells_own = bf16[512,1024]{1,0:T(8,128)(2,1)} custom-call(s32[1]{0:T(128)} %bitcast.flip, f32[4,128,1024]{2,1,0:T(8,128)} %tangent.5, bf16[528,1024]{1,0:T(8,128)(2,1)} %pack.1.own, bf16[528,1024]{1,0:T(8,128)(2,1)} %copy-done.1, bf16[528,1024]{1,0:T(8,128)(2,1)} %copy-done, f32[1,1024]{1,0:T(1,128)} %bitcast.15, ...), custom_call_target="tpu_custom_call" | custom-call | tf_op jit(solution)/shard_map/observe/pallas_call | solution.py:464
  58.9 0.1 collective-permute-start.3
  59.0 1.9 %collective-permute-start.2 = (bf16[512,1024]{1,0:T(8,128)(2,1)}, bf16[512,1024]{1,0:T(8,128)(2,1)S(1)}, u32[]{:S(2)}, u32[]{:S(2)}) collective-permute-start(bf16[512,1024]{1,0:T(8,128)(2,1)} %observe.1.cells_own), channel_id=1, source_target_pairs={{1,2},{3,4},{5,6},{7,8},{9,10},{11,12},{13,14},{2,1},{4,3},{6,5},{... | collective-permute-start | bytes 3145736 | tf_op jit(solution)/shard_map/ppermute | solution.py:498
  60.9 0.9 collective-permute-done.3.cells_near
  61.9 0.0 copy-start.5
  61.9 1.0 copy-done.5
  62.8 7.4 %near_adjoint.1 = (f32[256,1024]{1,0:T(8,128)}, f32[256,1024]{1,0:T(8,128)}, f32[256,1024]{1,0:T(8,128)}) custom-call(s32[1]{0:T(128)} %bitcast.flip, bf16[512,1024]{1,0:T(8,128)(2,1)} %observe.1.cells_own, bf16[512,1024]{1,0:T(8,128)(2,1)} %copy-done.5, bf16[528,1024]{1,0:T(8,128)(2,1)} %pack.1.own, bf16[528,1024]{1,0:T(8,128)(2,1)} %copy-done.1, ...), custom_call_target="tpu_custom_call" | custom-call | flops 2000000000 | bytes 8000000 | tf_op jit(solution)/shard_map/near_adjoint/pallas_call | solution.py:500
  70.2 16.4 %collective-permute-done.2.cells_far = bf16[512,1024]{1,0:T(8,128)(2,1)S(1)} collective-permute-done((bf16[512,1024]{1,0:T(8,128)(2,1)}, bf16[512,1024]{1,0:T(8,128)(2,1)S(1)}, u32[]{:S(2)}, u32[]{:S(2)}) %collective-permute-start.2) | collective-permute-done | bytes 1048608 | tf_op jit(solution)/shard_map/ppermute | solution.py:498
  86.6 0.0 copy-start.2
  86.6 1.0 %copy-done.2 = bf16[512,1024]{1,0:T(8,128)(2,1)} copy-done((bf16[512,1024]{1,0:T(8,128)(2,1)}, bf16[512,1024]{1,0:T(8,128)(2,1)S(1)}, u32[]{:S(2)}) %copy-start.2) | copy-done | bytes 1048600
  87.5 9.9 %far_adjoint.1 = f32[4,128,1024]{2,1,0:T(8,128)} custom-call(s32[1]{0:T(128)} %bitcast.flip, bf16[512,1024]{1,0:T(8,128)(2,1)} %observe.1.cells_own, bf16[512,1024]{1,0:T(8,128)(2,1)} %copy-done.2, bf16[528,1024]{1,0:T(8,128)(2,1)} %pack.1.own, bf16[528,1024]{1,0:T(8,128)(2,1)} %copy-done, f32[1,1024]{1,0:T(1,128)} %bitcast.17, ...), custom_call_target="tpu_custom_call" | custom-call | tf_op jit(solution)/shard_map/far_adjoint/pallas_call | solution.py:517
  (1 shorter events, 0.0 us)
Async XLA Ops:
  0.0 9.1 %copy-start.4 = (bf16[1,480]{1,0:T(2,128)(2,1)S(1)}, bf16[1,480]{1,0:T(2,128)(2,1)}, u32[]{:S(2)}) copy-start(bf16[1,480]{1,0:T(2,128)(2,1)} %param.16) | copy-start | bytes 2884
  0.0 9.9 %copy-start.3 = (s32[1,480]{1,0:T(1,128)S(1)}, s32[1,480]{1,0:T(1,128)}, u32[]{:S(2)}) copy-start(s32[1,480]{1,0:T(1,128)} %param.14) | copy-start | bytes 5764
  4.6 7.6 %collective-permute-start = (bf16[528,1024]{1,0:T(8,128)(2,1)}, bf16[528,1024]{1,0:T(8,128)(2,1)S(1)}, u32[]{:S(2)}, u32[]{:S(2)}) collective-permute-start(bf16[528,1024]{1,0:T(8,128)(2,1)} %pack.1.own), channel_id=1, source_target_pairs={{0,1},{1,0},{2,3},{3,2},{4,5},{5,4},{6,7},{7,6},{8,9},{9,8},{10,11... | collective-permute-start | bytes 3244040 | tf_op jit(solution)/shard_map/ppermute | solution.py:426
  6.1 28.3 %collective-permute-start.1 = (bf16[528,1024]{1,0:T(8,128)(2,1)}, bf16[528,1024]{1,0:T(8,128)(2,1)S(1)}, u32[]{:S(2)}, u32[]{:S(2)}) collective-permute-start(bf16[528,1024]{1,0:T(8,128)(2,1)} %pack.1.own), channel_id=1, source_target_pairs={{1,2},{3,4},{5,6},{7,8},{9,10},{11,12},{13,14},{2,1},{4,3},{6,5},{... | collective-permute-start | bytes 3244040 | tf_op jit(solution)/shard_map/ppermute | solution.py:427
  12.3 1.0 %copy-start.1 = (bf16[528,1024]{1,0:T(8,128)(2,1)}, bf16[528,1024]{1,0:T(8,128)(2,1)S(1)}, u32[]{:S(2)}) copy-start(bf16[528,1024]{1,0:T(8,128)(2,1)S(1)} %collective-permute-done.near) | copy-start | bytes 3244036
  34.3 1.0 copy-start
  58.9 2.9 %collective-permute-start.3 = (bf16[512,1024]{1,0:T(8,128)(2,1)}, bf16[512,1024]{1,0:T(8,128)(2,1)S(1)}, u32[]{:S(2)}, u32[]{:S(2)}) collective-permute-start(bf16[512,1024]{1,0:T(8,128)(2,1)} %observe.1.cells_own), channel_id=1, source_target_pairs={{0,1},{1,0},{2,3},{3,2},{4,5},{5,4},{6,7},{7,6},{8,9},{9,8},{10,11... | collective-permute-start | bytes 3145736 | tf_op jit(solution)/shard_map/ppermute | solution.py:497
  59.0 27.6 %collective-permute-start.2 = (bf16[512,1024]{1,0:T(8,128)(2,1)}, bf16[512,1024]{1,0:T(8,128)(2,1)S(1)}, u32[]{:S(2)}, u32[]{:S(2)}) collective-permute-start(bf16[512,1024]{1,0:T(8,128)(2,1)} %observe.1.cells_own), channel_id=1, source_target_pairs={{1,2},{3,4},{5,6},{7,8},{9,10},{11,12},{13,14},{2,1},{4,3},{6,5},{... | collective-permute-start | bytes 3145736 | tf_op jit(solution)/shard_map/ppermute | solution.py:498
  61.9 1.0 copy-start.5
  86.6 1.0 %copy-start.2 = (bf16[512,1024]{1,0:T(8,128)(2,1)}, bf16[512,1024]{1,0:T(8,128)(2,1)S(1)}, u32[]{:S(2)}) copy-start(bf16[512,1024]{1,0:T(8,128)(2,1)S(1)} %collective-permute-done.2.cells_far) | copy-start | bytes 3145732
where the time goes:
time: 97.8 us; the launch traced here: 97.5 us
  Pallas kernels  58.8 us (60%)
  waiting for transfers between devices  23.8 us (24%)
  starting transfers between devices  6.47 us (7%)
  local copies, waits for them, and re-layouts  4.94 us (5%)
  other arithmetic  2.78 us (3%)
    pallas_call x1, Pallas kernels, local(): pl.pallas_call(observe_kernel, out_shape=jax.ShapeDtypeStruct((cells, lev...  23.6 us
    ppermute x1, waiting for transfers between devices, local(): cells_far = lax.ppermute(cells_own, 'lat', links)  16.4 us
    pallas_call x1, Pallas kernels, local(): pl.pallas_call(near_kernel, out_shape=[slope_shape, slope_shape] + kept_s...  14.6 us
    pallas_call x1, Pallas kernels, local(): pl.pallas_call(far_adjoint_kernel, out_shape=jax.ShapeDtypeStruct((rows,...  9.94 us
    pallas_call x1, Pallas kernels, local(): pl.pallas_call(near_adjoint_kernel, out_shape=kept_shape, in_specs=[SMEM]...  7.36 us
    ppermute x1, waiting for transfers between devices, local(): far = lax.ppermute(own, 'lat', links)  6.47 us
    unnamed x12, local copies, waits for them, and re-layouts  3.92 us
    pallas_call x1, Pallas kernels, local(): pl.pallas_call(pack_kernel, out_shape=jax.ShapeDtypeStruct((cells + steps...  3.27 us
  transfers between devices with their start and end apart: 4, of which 3 were waited for; matrix products, arithmetic and copies ran while one was open for 3% of the time, Pallas kernels for 23%

commit v1 on v0

v1 whole, which is shorter than its diff:
```python
import functools

import jax
import jax.numpy as jnp
from jax import lax
from jax.experimental import pallas as pl
from jax.experimental.pallas import tpu as pltpu
from jax.sharding import PartitionSpec as P

F32 = jnp.float32
BF16 = jnp.bfloat16
FAR_CELLS = 304
FAR_COLUMNS = 272
ANY = pl.BlockSpec(memory_space=pl.ANY)
VMEM = pl.BlockSpec(memory_space=pltpu.VMEM)
HBM = pl.BlockSpec(memory_space=pltpu.HBM)
SMEM = pl.BlockSpec(memory_space=pltpu.SMEM)
VMEM_LIMIT = 28 * 1024 * 1024


def dot_t(left, right):
    return lax.dot_general(left, right, (((1,), (1,)), ((), ())), preferred_element_type=F32)


def dot(left, right):
    return jnp.dot(left, right, preferred_element_type=F32)


def store_sources(table, slot, codes, mirrored, sign, lon, rows):
    code = codes.astype(F32) - 1.0
    lat_q = jnp.where(code >= 5.0, 1.0, 0.0) + jnp.where(code >= 10.0, 1.0, 0.0)
    lon_step = code - 5.0 * lat_q - 2.0
    col = lax.broadcasted_iota(jnp.int32, code.shape, 1).astype(F32) - lon_step
    col = jnp.where(col < 0.0, col + lon, jnp.where(col >= lon, col - lon, col))
    stored = lax.broadcasted_iota(jnp.int32, code.shape, 0) & (rows - 1)
    row = (rows - 1 - stored) if mirrored else stored
    row = (row + slot * rows).astype(F32)
    src = (row - sign * (lat_q - 1.0)) * lon + col
    table[slot * code.shape[0] : (slot + 1) * code.shape[0], :] = jnp.where(code < 0.0, -65536.0, src)


def table_row(step, ext, rows):
    slot, at = ext // rows, ext % rows
    return slot * rows * rows + step * rows + (at if slot == 1 else rows - 1 - at)


def pull_matrix(out, turned, step, ext, lon, rows):
    span = 4 * lon
    lanes = lax.broadcasted_iota(jnp.int32, (lon, span), 1).astype(F32) + float((ext - 1) * lon)
    for half in range(2):
        k = table_row(step, ext + half, rows)
        column = turned[:, k : k + 1]
        out[half * lon : (half + 1) * lon, :] = jnp.where(column == lanes, 1.0, 0.0).astype(BF16)


def push_matrix(out, table, step, ext, lon, rows):
    dest = lax.broadcasted_iota(jnp.int32, (2 * lon, lon), 0).astype(F32) + float(ext * lon)
    for part in range(4):
        k = table_row(step, ext - 1 + part, rows)
        line = table[k : k + 1, :]
        out[:, part * lon : (part + 1) * lon] = jnp.where(line == dest, 1.0, 0.0).astype(BF16)


def wind_fields(codes, sign, rows):
    code = codes.astype(F32) - 1.0
    lat_q = jnp.where(code >= 5.0, 1.0, 0.0) + jnp.where(code >= 10.0, 1.0, 0.0)
    lat = jnp.where(code < 0.0, 9.0, sign * (lat_q - 1.0))
    lon = code - 5.0 * lat_q - 2.0
    fill = jnp.full((8 - rows, code.shape[1]), 9.0, F32)
    fields = []
    for step in range(code.shape[0] // rows):
        at = slice(step * rows, (step + 1) * rows)
        fields.append((jnp.concatenate([lat[at], fill], axis=0), jnp.concatenate([lon[at], fill], axis=0)))
    return fields


def shift_rows(mask, by):
    blank = jnp.zeros((1, mask.shape[1]), F32)
    if by == 1:
        return jnp.concatenate([blank, mask[:-1]], axis=0)
    if by == -1:
        return jnp.concatenate([mask[1:], blank], axis=0)
    return mask


def cells_pulled(fields, rows):
    lon = fields[0][0].shape[1]
    row = lax.broadcasted_iota(jnp.int32, (8, lon), 0)
    mask = jnp.where(row == 0, 1.0, 0.0)
    for lat, east in reversed(fields[: len(fields) - 1]):
        new = mask
        for a in (-1, 0, 1):
            total = jnp.zeros_like(mask)
            for b in range(-2, 3):
                hit = jnp.where((lat == float(a)) & (east == float(b)), mask, 0.0)
                total = jnp.maximum(total, hit if b == 0 else pltpu.roll(hit, (-b) % lon, 1))
            new = jnp.maximum(new, shift_rows(total, -a))
        mask = jnp.where(row < rows, new, 0.0)
    return mask


def cells_reached(fields, rows):
    lon = fields[0][0].shape[1]
    row = lax.broadcasted_iota(jnp.int32, (8, lon), 0)
    mask = jnp.zeros((8, lon), F32)
    for lat, east in fields:
        new = mask
        for a in (-1, 0, 1):
            source = shift_rows(mask, a)
            if a == 1:
                source = jnp.where(row == 0, 1.0, source)
            for b in range(-2, 3):
                seen = source if b == 0 else pltpu.roll(source, b % lon, 1)
                new = jnp.maximum(new, jnp.where((lat == float(a)) & (east == float(b)), seen, 0.0))
        mask = jnp.where(row < rows, new, 0.0)
    return mask


def slot_of(mask):
    lon = mask.shape[1]
    before = lax.broadcasted_iota(jnp.int32, (lon, lon), 0) < lax.broadcasted_iota(jnp.int32, (lon, lon), 1)
    place = dot(mask.astype(BF16), jnp.where(before, 1.0, 0.0).astype(BF16))
    totals = jnp.sum(mask, axis=1, keepdims=True)
    ahead = jnp.zeros((1, 1), F32)
    lines = []
    for j in range(mask.shape[0]):
        lines.append(place[j : j + 1] + ahead)
        ahead = ahead + totals[j : j + 1]
    return jnp.where(mask > 0.0, jnp.concatenate(lines, axis=0), -1.0), ahead


def choose_matrix(slots, size, rows, first=0):
    lon = slots.shape[1]
    at = lax.broadcasted_iota(jnp.int32, (size, lon), 0).astype(F32) + float(first)
    parts = [jnp.where(slots[j : j + 1] == at, 1.0, 0.0) for j in range(rows)]
    return jnp.concatenate(parts, axis=1).astype(BF16)


def spread_matrix(turned, row, size, first=0):
    at = lax.broadcasted_iota(jnp.int32, (turned.shape[0], size), 1).astype(F32) + float(first)
    return jnp.where(turned[:, row : row + 1] == at, 1.0, 0.0).astype(BF16)


def turn(slots):
    lon = slots.shape[1]
    return jnp.concatenate([slots, jnp.full((lon - slots.shape[0], lon), -1.0, F32)], axis=0).T


def sign_of(flip):
    return jnp.where(flip[0] == 1, -1.0, 1.0)


def pack_kernel(flip, tangent, wind, own, sent, slots, over, buf, codes, sem):
    rows, lon = tangent.shape[0], tangent.shape[1]
    cells = rows * lon
    copies = []
    for j in range(rows):
        at = jnp.where(flip[0] == 1, rows - 1 - j, j)
        copies.append(pltpu.make_async_copy(tangent.at[at], buf.at[j], sem.at[j]))
        copies[-1].start()
    for step in range(wind.shape[0]):
        for j in range(rows):
            code = jnp.where(flip[0] == 1, wind[step, rows - 1 - j : rows - j, :], wind[step, j : j + 1, :])
            codes[step * rows + j : step * rows + j + 1, :] = code.astype(F32) + 1.0
    mask = cells_pulled(wind_fields(codes[...], sign_of(flip), rows), rows)
    where, total = slot_of(mask)
    slots[...] = where
    capacity = sent.shape[0] - codes.shape[0]
    flag = jnp.where(total > float(capacity), 1.0, 0.0)
    over[...] = jnp.broadcast_to(flag, over.shape)
    head = codes.shape[0]
    tall = jnp.concatenate([mask, jnp.zeros((head - mask.shape[0], lon), F32)], axis=0)
    notes = jnp.concatenate(
        [codes[...], tall, jnp.broadcast_to(flag, (head, lon)), jnp.zeros((head, own.shape[1] - 3 * lon), F32)], axis=1
    ).astype(BF16)
    own[cells:, :] = notes
    sent[capacity:, :] = notes
    choose = choose_matrix(where, capacity, rows)
    for j in range(rows):
        copies[j].wait()
        own[j * lon : (j + 1) * lon, :] = buf[j].astype(BF16)
    sent[0:capacity, :] = dot(choose, own[0:cells, :]).astype(BF16)


def rest_kernel(first, slots, dense, out):
    rows = dense.shape[0] // slots.shape[1]
    cells = rows * slots.shape[1]
    choose = choose_matrix(slots[...], out.shape[0], rows, first)
    out[...] = dot(choose, dense[0:cells, :]).astype(BF16)


def blank_kernel(out):
    pass


def near_steps(mats, start_b, start_f, c_ref, outs, mid_b, mid_f, lon):
    c = c_ref[0:1, :]
    blocks = ((5, 7, 9), (6, 8), (7,))
    read_b, read_f, first = start_b, start_f, 4
    k = 0
    for step, exts in enumerate(blocks):
        for ext in exts:
            at = (ext - 1 - first) * lon
            pulled = dot(mats[k], read_b(at, 4 * lon))
            value = (1.0 - c) * read_f(at + lon, 2 * lon) + c * pulled
            k += 1
            if ext == exts[0]:
                outs[step][...] = value
            if step < 2:
                to = (ext - exts[0]) * lon
                mid_f[step, to : to + 2 * lon, :] = value
                mid_b[step, to : to + 2 * lon, :] = value.astype(BF16)
        first = exts[0]
        read_b = functools.partial(lambda s, a, n: mid_b[s, a : a + n, :], step)
        read_f = functools.partial(lambda s, a, n: mid_f[s, a : a + n, :], step)


def far_steps(mats, start_b, start_f, c_ref, kept, mid_b, mid_f, lon, finish):
    c = c_ref[0:1, :]
    k = 0
    for step in range(4):
        now, last = step % 2, (step + 1) % 2
        for half in range(2):
            at = 2 * half * lon
            if step == 0:
                window, own = start_b(at, 4 * lon), start_f(at + lon, 2 * lon)
            else:
                window = mid_b[last, at : at + 4 * lon, :]
                own = mid_f[last, at + lon : at + 3 * lon, :]
            value = (1.0 - c) * own + c * dot(mats[k], window)
            k += 1
            if step < 3:
                mid_f[now, at : at + 2 * lon, :] = value
                mid_b[now, at : at + 2 * lon, :] = value.astype(BF16)
            else:
                finish(half, value)
        if step < 3:
            carried = kept[step][...]
            mid_f[now, 4 * lon :, :] = carried
            mid_b[now, 4 * lon :, :] = carried.astype(BF16)


def near_kernel(
    flip, tangent, own, near, courant, background, w_first, w_second, where_col, where_row,
    slope_one, slope_two, kept_a, kept_b, kept_c, pick, place, place_far, slots,
    table, mats, cells_b, mid_b, mid_f, hidden,
):
    rows, lon = tangent.shape[0], tangent.shape[1]
    cells = rows * lon
    sign = sign_of(flip)
    table[...] = jnp.zeros_like(table)
    store_sources(table, 1, own[cells:, 0:lon], False, sign, lon, rows)
    store_sources(table, 2, near[cells:, 0:lon], True, sign, lon, rows)
    turned = table[...].T
    k = 0
    for step, exts in enumerate(((5, 7, 9), (6, 8), (7,))):
        for ext in exts:
            pull_matrix(mats.at[k], turned, step, ext, lon, rows)
            k += 1
    cells_b[0:cells, :] = own[0:cells, :]
    for j in range(rows):
        cells_b[(rows + j) * lon : (rows + j + 1) * lon, :] = near[(rows - 1 - j) * lon : (rows - j) * lon, :]

    def start_f(at, size):
        pieces = []
        for row in range(at // lon, (at + size) // lon):
            if row < rows:
                pieces.append(tangent[jnp.where(flip[0] == 1, rows - 1 - row, row)])
            else:
                pieces.append(cells_b[row * lon : (row + 1) * lon, :].astype(F32))
        return jnp.concatenate(pieces, axis=0)

    near_steps(
        mats, lambda at, size: cells_b[at : at + size, :], start_f, courant,
        (kept_a, kept_b, kept_c), mid_b, mid_f, lon,
    )

    first_tanh = jnp.tanh(dot(background[...], w_first[...]))
    hidden[...] = first_tanh.astype(BF16)
    slope_one[...] = 1.0 - first_tanh * first_tanh
    second_tanh = jnp.tanh(dot(hidden[...], w_second[...]))
    slope_two[...] = 1.0 - second_tanh * second_tanh

    count = where_col.shape[0]
    pick[...] = jnp.where(
        where_col[...] == lax.broadcasted_iota(jnp.int32, (count, cells), 1), 1.0, 0.0
    ).astype(BF16)
    place[...] = jnp.where(
        where_row[...] == lax.broadcasted_iota(jnp.int32, (cells, count), 0), 1.0, 0.0
    ).astype(BF16)
    where, _ = slot_of(cells_reached(wind_fields(own[cells:, 0:lon], sign, rows), rows))
    slots[...] = where
    place_far[...] = dot(choose_matrix(where, place_far.shape[0], rows), place[...]).astype(BF16)


def observe_kernel(
    flip, flag, tangent, own, far, rest, courant, slope_one, slope_two, kept_a, kept_b, kept_c,
    w_first, w_second, w_third, pick, place, place_far, quality, chan_weight,
    out, sent,
    table, mats, cells_b, mid_b, mid_f, last_b, one_b, two_b, rest_b, sem,
):
    rows, lon = tangent.shape[0], tangent.shape[1]
    cells = rows * lon
    sign = sign_of(flip)
    capacity = far.shape[0] - (own.shape[0] - cells)
    table[...] = jnp.zeros_like(table)
    store_sources(table, 0, far[capacity:, 0:lon], True, sign, lon, rows)
    store_sources(table, 1, own[cells:, 0:lon], False, sign, lon, rows)
    turned = table[...].T
    for step in range(4):
        for half in range(2):
            pull_matrix(mats.at[2 * step + half], turned, step, step + 1 + 2 * half, lon, rows)
    where, _ = slot_of(far[capacity:, lon : 2 * lon].astype(F32)[0:8])
    where = turn(where)
    for j in range(rows):
        value = dot(spread_matrix(where, j, capacity), far[0:capacity, :])
        cells_b[(rows - 1 - j) * lon : (rows - j) * lon, :] = value.astype(BF16)
    cells_b[cells:, :] = own[0 : 2 * lon, :]

    @pl.when(flag[0] > 0)
    def _():
        copy = pltpu.make_async_copy(rest, rest_b, sem.at[0])
        copy.start()
        copy.wait()
        for j in range(rows):
            value = dot(spread_matrix(where, j, rest_b.shape[0], capacity), rest_b[...])
            at = slice((rows - 1 - j) * lon, (rows - j) * lon)
            cells_b[at, :] = (cells_b[at, :].astype(F32) + value).astype(BF16)

    def start_f(at, size):
        pieces = []
        for row in range(at // lon, (at + size) // lon):
            if row == rows:
                pieces.append(tangent[jnp.where(flip[0] == 1, rows - 1, 0)])
            else:
                pieces.append(cells_b[row * lon : (row + 1) * lon, :].astype(F32))
        return jnp.concatenate(pieces, axis=0)

    def finish(half, value):
        last_b[2 * half * lon : 2 * (half + 1) * lon, :] = value.astype(BF16)

    far_steps(
        mats, lambda at, size: cells_b[at : at + size, :], start_f, courant,
        (kept_a, kept_b, kept_c), mid_b, mid_f, lon, finish,
    )
    one_b[...] = dot(pick[...], last_b[...]).astype(BF16)
    two_b[...] = (slope_one[...] * dot(one_b[...], w_first[...])).astype(BF16)
    one_b[...] = (slope_two[...] * dot(two_b[...], w_second[...])).astype(BF16)
    scale = quality[...] * chan_weight[0:1, :]
    two_b[...] = (scale * dot(one_b[...], w_third[...])).astype(BF16)
    one_b[...] = (slope_two[...] * dot_t(two_b[...], w_third[...])).astype(BF16)
    two_b[...] = (slope_one[...] * dot_t(one_b[...], w_second[...])).astype(BF16)
    one_b[...] = dot_t(two_b[...], w_first[...]).astype(BF16)
    sent[...] = dot(place_far[...], one_b[...]).astype(BF16)
    out[...] = dot(place[...], one_b[...]).astype(BF16)


def near_adjoint_kernel(
    flip, cells_own, cells_near, own, near, far, own_slots, courant,
    kept_a, kept_b, kept_c, far_mats, spread, far_slots, over,
    table, mats, cells_b, mid_b, mid_f,
):
    rows, lon = 4, table.shape[1]
    cells = rows * lon
    sign = sign_of(flip)
    head = own.shape[0] - cells
    far_codes = far[far.shape[0] - head :, 0:lon]
    store_sources(table, 0, far_codes, True, sign, lon, rows)
    store_sources(table, 1, own[cells:, 0:lon], False, sign, lon, rows)
    store_sources(table, 2, near[cells:, 0:lon], True, sign, lon, rows)
    k = 0
    for order, exts in enumerate(((5, 7, 9), (6, 8), (7,))):
        for ext in exts:
            push_matrix(mats.at[k], table, 3 - order, ext, lon, rows)
            k += 1
    cells_b[0:cells, :] = cells_own[...]
    for j in range(rows):
        cells_b[(rows + j) * lon : (rows + j + 1) * lon, :] = cells_near[
            (rows - 1 - j) * lon : (rows - j) * lon, :
        ]
    near_steps(
        mats, lambda at, size: cells_b[at : at + size, :],
        lambda at, size: cells_b[at : at + size, :].astype(F32), courant,
        (kept_a, kept_b, kept_c), mid_b, mid_f, lon,
    )
    for order in range(4):
        for half in range(2):
            push_matrix(far_mats.at[2 * order + half], table, 3 - order, order + 1 + 2 * half, lon, rows)
    where, total = slot_of(cells_reached(wind_fields(far_codes, -sign, rows), rows))
    far_slots[...] = where
    where = turn(where)
    capacity = spread.shape[1]
    for j in range(rows):
        spread[j * lon : (j + 1) * lon, :] = spread_matrix(where, j, capacity)
    most = jnp.maximum(jnp.max(own_slots[...], axis=(0, 1), keepdims=True) + 1.0, total)
    over[...] = jnp.broadcast_to(jnp.where(most > float(capacity), 1.0, 0.0), over.shape)


def far_adjoint_kernel(
    flip, flag, cells_own, far, rest, courant, kept_a, kept_b, kept_c, mats, spread, far_slots,
    out,
    cells_b, mid_b, mid_f, result, rest_b, sem,
):
    rows, lon = out.shape[0], out.shape[1]
    cells = rows * lon
    for j in range(rows):
        value = dot(spread[j * lon : (j + 1) * lon, :], far[...])
        cells_b[(rows - 1 - j) * lon : (rows - j) * lon, :] = value.astype(BF16)
    cells_b[cells:, :] = cells_own[0 : 2 * lon, :]

    @pl.when(flag[0] > 0)
    def _():
        copy = pltpu.make_async_copy(rest, rest_b, sem.at[rows])
        copy.start()
        copy.wait()
        where = turn(far_slots[...])
        for j in range(rows):
            value = dot(spread_matrix(where, j, rest_b.shape[0], spread.shape[1]), rest_b[...])
            at = slice((rows - 1 - j) * lon, (rows - j) * lon)
            cells_b[at, :] = (cells_b[at, :].astype(F32) + value).astype(BF16)

    copies = []

    def finish(half, value):
        for part in range(2):
            j = 2 * half + part
            result[j] = value[part * lon : (part + 1) * lon, :]
            at = jnp.where(flip[0] == 1, rows - 1 - j, j)
            copies.append(pltpu.make_async_copy(result.at[j], out.at[at], sem.at[j]))
            copies[-1].start()

    far_steps(
        mats, lambda at, size: cells_b[at : at + size, :],
        lambda at, size: cells_b[at : at + size, :].astype(F32), courant,
        (kept_a, kept_b, kept_c), mid_b, mid_f, lon, finish,
    )
    for copy in copies:
        copy.wait()


def params():
    return pltpu.CompilerParams(vmem_limit_bytes=VMEM_LIMIT)


def shape(dims, dtype):
    return jax.ShapeDtypeStruct(dims, dtype)


def second_exchange(flag, first, slots, dense, size, links):
    out = shape((size, dense.shape[1]), BF16)

    def send():
        rest = pl.pallas_call(
            functools.partial(rest_kernel, first),
            out_shape=out,
            in_specs=[VMEM, VMEM],
            out_specs=VMEM,
            compiler_params=params(),
            name="rest",
        )(slots, dense)
        return lax.ppermute(rest, "lat", links)

    def skip():
        return pl.pallas_call(blank_kernel, out_shape=out, out_specs=ANY, name="blank")()

    return lax.cond(flag, send, skip)


def local(
    tangent,
    wind_code,
    courant,
    obs_index,
    obs_count,
    obs_quality,
    background,
    w_first,
    w_second,
    w_third,
    chan_weight,
):
    rows, lon, levels = tangent.shape
    cells = rows * lon
    head = wind_code.shape[0] * rows
    listed = obs_index.shape[1]
    hidden_size = w_first.shape[1]
    count = lax.axis_size("lat")
    here = lax.axis_index("lat")
    odd = (here % 2).astype(jnp.int32)
    flip = odd.reshape(1)
    linked = (here > 0) & (here < count - 1)
    pairs = [(i, i ^ 1) for i in range(count)]
    links = [(i, i + 1) for i in range(1, count - 1, 2)]
    links = links + [(b, a) for a, b in links]

    own, sent, slots, over = pl.pallas_call(
        pack_kernel,
        out_shape=[
            shape((cells + head, levels), BF16),
            shape((FAR_CELLS + head, levels), BF16),
            shape((8, lon), F32),
            shape((8, lon), F32),
        ],
        in_specs=[SMEM, HBM, VMEM],
        out_specs=[VMEM] * 4,
        scratch_shapes=[
            pltpu.VMEM((rows, lon, levels), F32),
            pltpu.VMEM((head, lon), F32),
            pltpu.SemaphoreType.DMA((rows,)),
        ],
        compiler_params=params(),
        name="pack",
    )(flip, tangent, wind_code)

    far = lax.ppermute(sent, "lat", links)
    near = lax.ppermute(own, "lat", pairs)

    c_row = courant.reshape(1, levels)
    slot_ids = jnp.arange(listed, dtype=jnp.int32)
    observed = slot_ids < obs_count[0]
    where_at = obs_index[0]
    where_at = jnp.where(odd == 1, where_at + (rows - 1 - 2 * (where_at // lon)) * lon, where_at)
    where_at = jnp.where(observed, where_at, -1)
    quality = jnp.where(observed, obs_quality[0].astype(F32), 0.0)

    kept_shape = [shape((2 * lon, levels), F32)] * 3
    slope_shape = shape((listed, hidden_size), F32)
    slope_one, slope_two, kept_a, kept_b, kept_c, pick, place, place_far, own_slots = pl.pallas_call(
        near_kernel,
        out_shape=[slope_shape, slope_shape]
        + kept_shape
        + [
            shape((listed, cells), BF16),
            shape((cells, listed), BF16),
            shape((FAR_COLUMNS, listed), BF16),
            shape((8, lon), F32),
        ],
        in_specs=[SMEM] + [VMEM] * 9,
        out_specs=[VMEM] * 9,
        scratch_shapes=[
            pltpu.VMEM((lon, lon), F32),
            pltpu.VMEM((6, 2 * lon, 4 * lon), BF16),
            pltpu.VMEM((2 * cells, levels), BF16),
            pltpu.VMEM((2, 6 * lon, levels), BF16),
            pltpu.VMEM((2, 6 * lon, levels), F32),
            pltpu.VMEM((listed, hidden_size), BF16),
        ],
        compiler_params=params(),
        cost_estimate=pl.CostEstimate(flops=4_000_000_000, bytes_accessed=16_000_000, transcendentals=1_000_000),
        name="near",
    )(
        flip, tangent, own, near, c_row, background[0], w_first, w_second,
        where_at.reshape(listed, 1), where_at.reshape(1, listed),
    )

    flag = linked & ((over[0, 0] > 0.0) | (far[FAR_CELLS, 2 * lon] > 0.0))
    rest = second_exchange(flag, FAR_CELLS, slots, own, cells - FAR_CELLS, links)
    cells_own, sent = pl.pallas_call(
        observe_kernel,
        out_shape=[shape((cells, levels), BF16), shape((FAR_COLUMNS, levels), BF16)],
        in_specs=[SMEM, SMEM, VMEM, VMEM, VMEM, ANY] + [VMEM] * 14,
        out_specs=[VMEM] * 2,
        scratch_shapes=[
            pltpu.VMEM((lon, lon), F32),
            pltpu.VMEM((8, 2 * lon, 4 * lon), BF16),
            pltpu.VMEM((6 * lon, levels), BF16),
            pltpu.VMEM((2, 6 * lon, levels), BF16),
            pltpu.VMEM((2, 6 * lon, levels), F32),
            pltpu.VMEM((cells, levels), BF16),
            pltpu.VMEM((listed, levels), BF16),
            pltpu.VMEM((listed, levels), BF16),
            pltpu.VMEM((cells - FAR_CELLS, levels), BF16),
            pltpu.SemaphoreType.DMA((1,)),
        ],
        compiler_params=params(),
        name="observe",
    )(
        flip, flag.astype(jnp.int32).reshape(1), tangent, own, far, rest, c_row,
        slope_one, slope_two, kept_a, kept_b, kept_c, w_first, w_second, w_third,
        pick, place, place_far, quality.reshape(listed, 1), chan_weight.reshape(1, -1),
    )

    columns_far = lax.ppermute(sent, "lat", links)
    cells_near = lax.ppermute(cells_own, "lat", pairs)

    kept_a, kept_b, kept_c, mats, spread, far_slots, over = pl.pallas_call(
        near_adjoint_kernel,
        out_shape=kept_shape
        + [
            shape((8, 2 * lon, 4 * lon), BF16),
            shape((cells, FAR_COLUMNS), BF16),
            shape((8, lon), F32),
            shape((8, lon), F32),
        ],
        in_specs=[SMEM] + [VMEM] * 7,
        out_specs=[VMEM] * 7,
        scratch_shapes=[
            pltpu.VMEM((lon, lon), F32),
            pltpu.VMEM((6, 2 * lon, 4 * lon), BF16),
            pltpu.VMEM((2 * cells, levels), BF16),
            pltpu.VMEM((2, 6 * lon, levels), BF16),
            pltpu.VMEM((2, 6 * lon, levels), F32),
        ],
        compiler_params=params(),
        cost_estimate=pl.CostEstimate(flops=2_000_000_000, bytes_accessed=8_000_000, transcendentals=0),
        name="near_adjoint",
    )(flip, cells_own, cells_near, own, near, far, own_slots, c_row)

    flag = linked & (over[0, 0] > 0.0)
    rest = second_exchange(flag, FAR_COLUMNS, own_slots, cells_own, cells - FAR_COLUMNS, links)
    return pl.pallas_call(
        far_adjoint_kernel,
        out_shape=shape((rows, lon, levels), F32),
        in_specs=[SMEM, SMEM, VMEM, VMEM, ANY] + [VMEM] * 7,
        out_specs=HBM,
        scratch_shapes=[
            pltpu.VMEM((6 * lon, levels), BF16),
            pltpu.VMEM((2, 6 * lon, levels), BF16),
            pltpu.VMEM((2, 6 * lon, levels), F32),
            pltpu.VMEM((rows, lon, levels), F32),
            pltpu.VMEM((cells - FAR_COLUMNS, levels), BF16),
            pltpu.SemaphoreType.DMA((rows + 1,)),
        ],
        compiler_params=params(),
        name="far_adjoint",
    )(
        flip, flag.astype(jnp.int32).reshape(1), cells_own, columns_far, rest, c_row,
        kept_a, kept_b, kept_c, mats, spread, far_slots,
    )


def solution(mesh):
    placed = (
        P(("groups", "lat"), None, None),
        P(None, ("groups", "lat"), None),
        P(),
        P(("groups", "lat"), None),
        P(("groups", "lat")),
        P(("groups", "lat"), None),
        P(("groups", "lat"), None, None),
        P(),
        P(),
        P(),
        P(),
    )
    return jax.shard_map(
        local,
        mesh=mesh,
        in_specs=placed,
        out_specs=P(("groups", "lat"), None, None),
        check_vma=False,
    )
```

time: 97.8 us -> 76.1 us (0.78)
  Pallas kernels: 58.8 us -> 32.6 us
  local copies, waits for them, and re-layouts: 4.94 us -> 14.2 us
  waiting for transfers between devices: 23.8 us -> 19.5 us
  other arithmetic: 2.78 us -> 0.26 us
  between operations: 0.75 us -> 3.04 us
    pallas_call x4 -> x6, Pallas kernels: 44.2 us -> 26.2 us  [the longest x1 13.2 us: local(): pl.pallas_call(observe_kernel, out_shape=[shape((cells, levels), BF16), s...]
    unnamed x12 -> x36, local copies, waits for them, and re-layouts: 3.92 us -> 12.2 us
    pallas_call x1, Pallas kernels: 14.6 us -> 6.32 us  [local(): pl.pallas_call(near_kernel, out_shape=[slope_shape, slope_shape] + kept_s...]
    ppermute x2, waiting for transfers between devices: 22.8 us -> 18.8 us  [the longest x1 13.4 us: local(): far = lax.ppermute(sent, 'lat', links)]
    slice x0 -> x3, local copies, waits for them, and re-layouts: none -> 1.68 us  [the longest x2 1.14 us: local(): flag = linked & ((over[0, 0] > 0.0) | (far[FAR_CELLS, 2 * lon] > 0.0))]
    select_n x2, other arithmetic: 1.44 us -> 0.23 us  [local(): where_at = jnp.where(observed, where_at, -1)]
  transfers between devices with their start and end apart: 4 -> 4, of which waited for: 3 -> 3; matrix products, arithmetic and copies ran while one was open for 3% -> 3% of each run, Pallas kernels for 23% -> 6%
where the time goes in v1:
time: 76.1 us; the launch traced here: 75.5 us
  Pallas kernels  32.6 us (43%)
  waiting for transfers between devices  19.5 us (26%)
  local copies, waits for them, and re-layouts  14.2 us (19%)
  starting transfers between devices  5.91 us (8%)
  between operations  3.04 us (4%)
    ppermute x1, waiting for transfers between devices, local(): far = lax.ppermute(sent, 'lat', links)  13.4 us
    pallas_call x1, Pallas kernels, local(): pl.pallas_call(observe_kernel, out_shape=[shape((cells, levels), BF16), s...  13.2 us
    unnamed x36, local copies, waits for them, and re-layouts  12.2 us
    pallas_call x1, Pallas kernels, local(): pl.pallas_call(near_kernel, out_shape=[slope_shape, slope_shape] + kept_s...  6.32 us
    pallas_call x1, Pallas kernels, local(): pl.pallas_call(far_adjoint_kernel, out_shape=shape((rows, lon, levels), F...  6.05 us
    ppermute x1, waiting for transfers between devices, local(): columns_far = lax.ppermute(sent, 'lat', links)  5.39 us
    pallas_call x1, Pallas kernels, local(): pl.pallas_call(near_adjoint_kernel, out_shape=kept_shape + [shape((8, 2 *...  4.85 us
    ppermute x1, starting transfers between devices, local(): far = lax.ppermute(sent, 'lat', links)  3.18 us
  transfers between devices with their start and end apart: 4, of which 3 were waited for; matrix products, arithmetic and copies ran while one was open for 3% of the time, Pallas kernels for 6%

profile of v1, /device:TPU:25, one launch (start us, length us, event | category | flops | bytes accessed | tf_op | source)
XLA Modules:
  0.0 75.5 jit_solution(15569297017072444767)
XLA Ops:
  0.0 0.0 copy-start.17
  0.0 0.0 copy-start.16
  0.0 0.0 copy-start
  0.0 1.6 %copy-done = f32[4,128,1024]{2,1,0:T(8,128)S(1)} copy-done((f32[4,128,1024]{2,1,0:T(8,128)S(1)}, f32[4,128,1024]{2,1,0:T(8,128)}, u32[]{:S(2)}) %copy-start) | copy-done | bytes 2097176
  1.6 0.0 copy-start.12
  1.6 0.7 copy-done.12
  2.3 2.1 %pack.1 = (bf16[528,1024]{1,0:T(8,128)(2,1)}, bf16[320,1024]{1,0:T(8,128)(2,1)}, f32[8,128]{1,0:T(8,128)S(1)}, f32[8,128]{1,0:T(8,128)S(1)}) custom-call(s32[1]{0:T(128)} %bitcast.flip, f32[4,128,1024]{2,1,0:T(8,128)S(1)} %copy-done, s32[4,4,128]{2,1,0:T(4,128)S(1)} %copy-done.12), custom_call_target="tpu_custom_call" | custom-call | tf_op jit(solution)/shard_map/pack/pallas_call | solution.py:496
  4.5 0.0 copy-start.1
  4.5 0.0 copy-start.11
  4.5 0.7 collective-permute-start.3
  5.2 3.2 %collective-permute-start.2 = (bf16[320,1024]{1,0:T(8,128)(2,1)}, bf16[320,1024]{1,0:T(8,128)(2,1)S(1)}, u32[]{:S(2)}, u32[]{:S(2)}) collective-permute-start(bf16[320,1024]{1,0:T(8,128)(2,1)} %get-tuple-element.46), channel_id=1, source_target_pairs={{1,2},{3,4},{5,6},{7,8},{9,10},{11,12},{13,14},{2,1},{4,3},{6,5},{... | collective-permute-start | bytes 1966088 | tf_op jit(solution)/shard_map/ppermute | solution.py:515
  9.1 0.0 copy-done.17
  9.1 0.1 copy.18
  9.2 0.0 copy-done.16
  9.3 0.1 copy.16
  9.4 0.6 slice.9
  10.7 0.2 fusion.4.where_col
  10.9 13.4 %collective-permute-done.2.far = bf16[320,1024]{1,0:T(8,128)(2,1)S(1)} collective-permute-done((bf16[320,1024]{1,0:T(8,128)(2,1)}, bf16[320,1024]{1,0:T(8,128)(2,1)S(1)}, u32[]{:S(2)}, u32[]{:S(2)}) %collective-permute-start.2) | collective-permute-done | bytes 655392 | tf_op jit(solution)/shard_map/ppermute | solution.py:515
  24.4 0.0 copy-start.9
  24.4 0.6 slice.12
  25.6 0.0 collective-permute-done.3.near
  25.6 0.0 copy-done.1
  25.6 0.0 copy-done.11
  25.6 0.0 copy-start.2
  25.6 1.6 %copy-done.2 = bf16[1024,1024]{1,0:T(8,128)(2,1)S(1)} copy-done((bf16[1024,1024]{1,0:T(8,128)(2,1)S(1)}, bf16[1024,1024]{1,0:T(8,128)(2,1)}, u32[]{:S(2)}) %copy-start.2) | copy-done | bytes 2097176
  27.2 0.0 copy-start.3
  27.2 1.6 %copy-done.3 = bf16[1024,1024]{1,0:T(8,128)(2,1)S(1)} copy-done((bf16[1024,1024]{1,0:T(8,128)(2,1)S(1)}, bf16[1024,1024]{1,0:T(8,128)(2,1)}, u32[]{:S(2)}) %copy-start.3) | copy-done | bytes 2097176
  28.8 1.2 %copy-done.14 = bf16[1,480,1024]{2,1,0:T(8,128)(2,1)S(1)} copy-done((bf16[1,480,1024]{2,1,0:T(8,128)(2,1)S(1)}, bf16[1,480,1024]{2,1,0:T(8,128)(2,1)}, u32[]{:S(2)}) %copy-start.14) | copy-done | bytes 983064
  30.0 6.3 %near.1 = (f32[480,1024]{1,0:T(8,128)S(1)}, f32[480,1024]{1,0:T(8,128)S(1)}, f32[256,1024]{1,0:T(8,128)S(1)}, f32[256,1024]{1,0:T(8,128)S(1)}, f32[256,1024]{1,0...) custom-call(s32[1]{0:T(128)} %bitcast.flip, ...), custom_call_target="tpu_custom_call" | custom-call | flops 4000000000 | bytes 16000000 | tf_op jit(solution)/shard_map/near/pallas_call | solution.py:528
  36.3 0.0 copy-done.9
  36.4 0.0 copy-done.4
  36.4 0.0 copy-done.13
  36.4 13.2 %observe.1 = (bf16[512,1024]{1,0:T(8,128)(2,1)S(1)}, bf16[272,1024]{1,0:T(8,128)(2,1)}) custom-call(s32[1]{0:T(128)} %bitcast.flip, s32[1]{0:T(128)} %bitcast.2.flag, f32[4,128,1024]{2,1,0:T(8,128)S(1)} %copy-done.1, bf16[528,1024]{1,0:T(8,128)(2,1)} %get-tuple-element.47.own, bf16[320,1024]{1,0:T(8,128)(2,1)S(1)} %collective-permute-done.2.far, ...), custom_call_target="tpu_custom_call" | custom-call | tf_op jit(solution)/shard_map/observe/pallas_call | solution.py:558
  49.6 0.0 copy-start.15
  49.6 0.1 collective-permute-start.4
  49.7 1.9 %collective-permute-start.5 = (bf16[272,1024]{1,0:T(8,128)(2,1)}, bf16[272,1024]{1,0:T(8,128)(2,1)}, u32[]{:S(2)}, u32[]{:S(2)}) collective-permute-start(bf16[272,1024]{1,0:T(8,128)(2,1)} %get-tuple-element.60), channel_id=1, source_target_pairs={{1,2},{3,4},{5,6},{7,8},{9,10},{11,12},{13,14},{2,1},{4,3},{6,5},{... | collective-permute-start | bytes 1671176 | tf_op jit(solution)/shard_map/ppermute | solution.py:583
  51.6 0.7 collective-permute-done.4.cells_near
  52.3 1.1 %copy-done.10 = bf16[320,1024]{1,0:T(8,128)(2,1)S(1)} copy-done((bf16[320,1024]{1,0:T(8,128)(2,1)S(1)}, bf16[320,1024]{1,0:T(8,128)(2,1)}, u32[]{:S(2)}) %copy-start.10) | copy-done | bytes 655384
  53.4 4.8 %near_adjoint.1 = (f32[256,1024]{1,0:T(8,128)S(1)}, f32[256,1024]{1,0:T(8,128)S(1)}, f32[256,1024]{1,0:T(8,128)S(1)}, bf16[8,256,512]{2,1,0:T(8,128)(2,1)S(1)}, ...) custom-call(s32[1]{0:T(128)} %bitcast.flip, ...), custom_call_target="tpu_custom_call" | custom-call | flops 2000000000 | bytes 8000000 | tf_op jit(solution)/shard_map/near_adjoint/pallas_call | solution.py:586
  58.3 0.0 copy-done.15
  58.3 0.0 copy-start.5
  58.3 1.0 %copy-done.5 = f32[256,1024]{1,0:T(8,128)} copy-done((f32[256,1024]{1,0:T(8,128)}, f32[256,1024]{1,0:T(8,128)S(1)}, u32[]{:S(2)}) %copy-start.5) | copy-done | bytes 1048600
  59.3 1.0 %copy-done.7 = f32[256,1024]{1,0:T(8,128)} copy-done((f32[256,1024]{1,0:T(8,128)}, f32[256,1024]{1,0:T(8,128)S(1)}, u32[]{:S(2)}) %copy-start.7) | copy-done | bytes 1048600
  60.2 0.5 slice.11
  61.4 5.4 %collective-permute-done.5.far = bf16[272,1024]{1,0:T(8,128)(2,1)} collective-permute-done((bf16[272,1024]{1,0:T(8,128)(2,1)}, bf16[272,1024]{1,0:T(8,128)(2,1)}, u32[]{:S(2)}, u32[]{:S(2)}) %collective-permute-start.5) | collective-permute-done | bytes 557088 | tf_op jit(solution)/shard_map/ppermute | solution.py:583
  66.8 1.2 %copy-done.6 = f32[256,1024]{1,0:T(8,128)S(1)} copy-done((f32[256,1024]{1,0:T(8,128)S(1)}, f32[256,1024]{1,0:T(8,128)}, u32[]{:S(2)}) %copy-start.6) | copy-done | bytes 1048600
  68.1 1.2 %copy-done.8 = f32[256,1024]{1,0:T(8,128)S(1)} copy-done((f32[256,1024]{1,0:T(8,128)S(1)}, f32[256,1024]{1,0:T(8,128)}, u32[]{:S(2)}) %copy-start.8) | copy-done | bytes 1048600
  69.3 6.0 %far_adjoint.1 = f32[4,128,1024]{2,1,0:T(8,128)} custom-call(s32[1]{0:T(128)} %bitcast.flip, s32[1]{0:T(128)} %bitcast.10.flag, bf16[512,1024]{1,0:T(8,128)(2,1)} %copy-done.15, bf16[272,1024]{1,0:T(8,128)(2,1)} %collective-permute-done.5.far, bf16[240,1024]{1,0:T(8,128)(2,1)} %get-tuple-element.68.rest, f32[1,1024]{1,0:T(1,128)S(1)} %bitcast.19, ...), custom_call_target="tpu_custom_call" | custom-call | tf_op jit(solution)/shard_map/far_adjoint/pallas_call | solution.py:611
  (14 shorter events, 0.1 us)
Async XLA Ops:
  0.0 9.1 %copy-start.17 = (bf16[1,480]{1,0:T(2,128)(2,1)S(1)}, bf16[1,480]{1,0:T(2,128)(2,1)}, u32[]{:S(2)}) copy-start(bf16[1,480]{1,0:T(2,128)(2,1)} %param.20) | copy-start | bytes 2884
  0.0 9.2 %copy-start.16 = (s32[1,480]{1,0:T(1,128)S(1)}, s32[1,480]{1,0:T(1,128)}, u32[]{:S(2)}) copy-start(s32[1,480]{1,0:T(1,128)} %param.18) | copy-start | bytes 5764
  0.0 1.6 %copy-start = (f32[4,128,1024]{2,1,0:T(8,128)S(1)}, f32[4,128,1024]{2,1,0:T(8,128)}, u32[]{:S(2)}) copy-start(f32[4,128,1024]{2,1,0:T(8,128)} %tangent.5) | copy-start | bytes 6291460
  1.6 0.7 copy-start.12
  4.5 21.1 %copy-start.1 = (f32[4,128,1024]{2,1,0:T(8,128)S(1)}, f32[4,128,1024]{2,1,0:T(8,128)}, u32[]{:S(2)}) copy-start(f32[4,128,1024]{2,1,0:T(8,128)} %tangent.5) | copy-start | bytes 6291460
  4.5 21.1 %copy-start.11 = (f32[1024]{0:T(1024)S(1)}, f32[1024]{0:T(1024)}, u32[]{:S(2)}) copy-start(f32[1024]{0:T(1024)} %param.17) | copy-start | bytes 12292
  4.5 21.1 %collective-permute-start.3 = (bf16[528,1024]{1,0:T(8,128)(2,1)}, bf16[528,1024]{1,0:T(8,128)(2,1)}, u32[]{:S(2)}, u32[]{:S(2)}) collective-permute-start(bf16[528,1024]{1,0:T(8,128)(2,1)} %get-tuple-element.47.own), channel_id=1, source_target_pairs={{0,1},{1,0},{2,3},{3,2},{4,5},{5,4},{6,7},{7,6},{8,9},{9,8},{10,11... | collective-permute-start | bytes 3244040 | tf_op jit(solution)/shard_map/ppermute | solution.py:516
  5.2 19.1 %collective-permute-start.2 = (bf16[320,1024]{1,0:T(8,128)(2,1)}, bf16[320,1024]{1,0:T(8,128)(2,1)S(1)}, u32[]{:S(2)}, u32[]{:S(2)}) collective-permute-start(bf16[320,1024]{1,0:T(8,128)(2,1)} %get-tuple-element.46), channel_id=1, source_target_pairs={{1,2},{3,4},{5,6},{7,8},{9,10},{11,12},{13,14},{2,1},{4,3},{6,5},{... | collective-permute-start | bytes 1966088 | tf_op jit(solution)/shard_map/ppermute | solution.py:515
  24.4 12.0 %copy-start.9 = (bf16[320,1024]{1,0:T(8,128)(2,1)}, bf16[320,1024]{1,0:T(8,128)(2,1)S(1)}, u32[]{:S(2)}) copy-start(bf16[320,1024]{1,0:T(8,128)(2,1)S(1)} %collective-permute-done.2.far) | copy-start | bytes 1966084
  25.6 1.6 %copy-start.2 = (bf16[1024,1024]{1,0:T(8,128)(2,1)S(1)}, bf16[1024,1024]{1,0:T(8,128)(2,1)}, u32[]{:S(2)}) copy-start(bf16[1024,1024]{1,0:T(8,128)(2,1)} %w_first.3) | copy-start | bytes 6291460
  27.2 1.6 %copy-start.3 = (bf16[1024,1024]{1,0:T(8,128)(2,1)S(1)}, bf16[1024,1024]{1,0:T(8,128)(2,1)}, u32[]{:S(2)}) copy-start(bf16[1024,1024]{1,0:T(8,128)(2,1)} %w_second.3) | copy-start | bytes 6291460
  28.8 1.2 %copy-start.14 = (bf16[1,480,1024]{2,1,0:T(8,128)(2,1)S(1)}, bf16[1,480,1024]{2,1,0:T(8,128)(2,1)}, u32[]{:S(2)}) copy-start(bf16[1,480,1024]{2,1,0:T(8,128)(2,1)} %param.21) | copy-start | bytes 2949124
  30.0 6.3 %copy-start.4 = (bf16[1024,1024]{1,0:T(8,128)(2,1)S(1)}, bf16[1024,1024]{1,0:T(8,128)(2,1)}, u32[]{:S(2)}) copy-start(bf16[1024,1024]{1,0:T(8,128)(2,1)} %w_third.1) | copy-start | bytes 6291460
  30.0 6.3 %copy-start.13 = (f32[1024]{0:T(1024)S(1)}, f32[1024]{0:T(1024)}, u32[]{:S(2)}) copy-start(f32[1024]{0:T(1024)} %param.25) | copy-start | bytes 12292
  49.6 8.7 %copy-start.15 = (bf16[512,1024]{1,0:T(8,128)(2,1)}, bf16[512,1024]{1,0:T(8,128)(2,1)S(1)}, u32[]{:S(2)}) copy-start(bf16[512,1024]{1,0:T(8,128)(2,1)S(1)} %get-tuple-element.57.cells_own) | copy-start | bytes 3145732
  49.6 2.7 %collective-permute-start.4 = (bf16[512,1024]{1,0:T(8,128)(2,1)S(1)}, bf16[512,1024]{1,0:T(8,128)(2,1)S(1)}, u32[]{:S(2)}, u32[]{:S(2)}) collective-permute-start(bf16[512,1024]{1,0:T(8,128)(2,1)S(1)} %get-tuple-element.57.cells_own), channel_id=1, source_target_pairs={{0,1},{1,0},{2,3},{3,2},{4,5},{5,4},{6,7},{7,6},{8,9},{9,8},{10,11... | collective-permute-start | bytes 3145736 | tf_op jit(solution)/shard_map/ppermute | solution.py:584
  49.7 17.1 %collective-permute-start.5 = (bf16[272,1024]{1,0:T(8,128)(2,1)}, bf16[272,1024]{1,0:T(8,128)(2,1)}, u32[]{:S(2)}, u32[]{:S(2)}) collective-permute-start(bf16[272,1024]{1,0:T(8,128)(2,1)} %get-tuple-element.60), channel_id=1, source_target_pairs={{1,2},{3,4},{5,6},{7,8},{9,10},{11,12},{13,14},{2,1},{4,3},{6,5},{... | collective-permute-start | bytes 1671176 | tf_op jit(solution)/shard_map/ppermute | solution.py:583
  52.3 1.1 %copy-start.10 = (bf16[320,1024]{1,0:T(8,128)(2,1)S(1)}, bf16[320,1024]{1,0:T(8,128)(2,1)}, u32[]{:S(2)}) copy-start(bf16[320,1024]{1,0:T(8,128)(2,1)} %copy-done.9) | copy-start | bytes 1966084
  58.3 1.0 %copy-start.5 = (f32[256,1024]{1,0:T(8,128)}, f32[256,1024]{1,0:T(8,128)S(1)}, u32[]{:S(2)}) copy-start(f32[256,1024]{1,0:T(8,128)S(1)} %get-tuple-element.62.kept_b) | copy-start | bytes 3145732
  59.3 1.0 %copy-start.7 = (f32[256,1024]{1,0:T(8,128)}, f32[256,1024]{1,0:T(8,128)S(1)}, u32[]{:S(2)}) copy-start(f32[256,1024]{1,0:T(8,128)S(1)} %get-tuple-element.63.kept_c) | copy-start | bytes 3145732
  66.8 1.2 %copy-start.6 = (f32[256,1024]{1,0:T(8,128)S(1)}, f32[256,1024]{1,0:T(8,128)}, u32[]{:S(2)}) copy-start(f32[256,1024]{1,0:T(8,128)} %copy-done.5) | copy-start | bytes 3145732
  68.1 1.2 %copy-start.8 = (f32[256,1024]{1,0:T(8,128)S(1)}, f32[256,1024]{1,0:T(8,128)}, u32[]{:S(2)}) copy-start(f32[256,1024]{1,0:T(8,128)} %copy-done.7) | copy-start | bytes 3145732

commit v2 on v1

--- a/solution.py
+++ b/solution.py
@@ -16,6 +16,7 @@
 HBM = pl.BlockSpec(memory_space=pltpu.HBM)
 SMEM = pl.BlockSpec(memory_space=pltpu.SMEM)
 VMEM_LIMIT = 28 * 1024 * 1024
+PACK_LIMIT = 60 * 1024 * 1024
 
 
 def dot_t(left, right):
@@ -150,29 +151,29 @@
     return jnp.where(flip[0] == 1, -1.0, 1.0)
 
 
-def pack_kernel(flip, tangent, wind, own, sent, slots, over, buf, codes, sem):
+def pack_kernel(flip, tangent, wind, own, sent, codes, slots, buf, wind_b, sem):
     rows, lon = tangent.shape[0], tangent.shape[1]
     cells = rows * lon
+    wind_copy = pltpu.make_async_copy(wind, wind_b, sem.at[rows])
+    wind_copy.start()
     copies = []
     for j in range(rows):
         at = jnp.where(flip[0] == 1, rows - 1 - j, j)
         copies.append(pltpu.make_async_copy(tangent.at[at], buf.at[j], sem.at[j]))
         copies[-1].start()
-    for step in range(wind.shape[0]):
+    wind_copy.wait()
+    for step in range(wind_b.shape[0]):
         for j in range(rows):
-            code = jnp.where(flip[0] == 1, wind[step, rows - 1 - j : rows - j, :], wind[step, j : j + 1, :])
+            code = jnp.where(flip[0] == 1, wind_b[step, rows - 1 - j : rows - j, :], wind_b[step, j : j + 1, :])
             codes[step * rows + j : step * rows + j + 1, :] = code.astype(F32) + 1.0
     mask = cells_pulled(wind_fields(codes[...], sign_of(flip), rows), rows)
-    where, total = slot_of(mask)
+    where, _ = slot_of(mask)
     slots[...] = where
-    capacity = sent.shape[0] - codes.shape[0]
-    flag = jnp.where(total > float(capacity), 1.0, 0.0)
-    over[...] = jnp.broadcast_to(flag, over.shape)
     head = codes.shape[0]
+    capacity = sent.shape[0] - head
     tall = jnp.concatenate([mask, jnp.zeros((head - mask.shape[0], lon), F32)], axis=0)
-    notes = jnp.concatenate(
-        [codes[...], tall, jnp.broadcast_to(flag, (head, lon)), jnp.zeros((head, own.shape[1] - 3 * lon), F32)], axis=1
-    ).astype(BF16)
+    notes = jnp.concatenate([codes[...], tall, jnp.zeros((head, own.shape[1] - 2 * lon), F32)], axis=1)
+    notes = notes.astype(BF16)
     own[cells:, :] = notes
     sent[capacity:, :] = notes
     choose = choose_matrix(where, capacity, rows)
@@ -180,6 +181,17 @@
         copies[j].wait()
         own[j * lon : (j + 1) * lon, :] = buf[j].astype(BF16)
     sent[0:capacity, :] = dot(choose, own[0:cells, :]).astype(BF16)
+
+
+def reach_kernel(flip, after, codes, pulled_slots, slots, over):
+    rows = 4
+    where, total = slot_of(cells_reached(wind_fields(codes[...], sign_of(flip), rows), rows))
+    slots[...] = where
+    pulled = jnp.max(pulled_slots[...], axis=(0, 1), keepdims=True) + 1.0
+    line = lax.broadcasted_iota(jnp.int32, over.shape, 1)
+    first = jnp.where(pulled > float(FAR_CELLS), 1.0, 0.0)
+    second = jnp.where(total > float(FAR_COLUMNS), 1.0, 0.0)
+    over[...] = jnp.where(line == 0, first, jnp.where(line == 1, second, 0.0))
 
 
 def rest_kernel(first, slots, dense, out):
@@ -241,24 +253,26 @@
 
 
 def near_kernel(
-    flip, tangent, own, near, courant, background, w_first, w_second, where_col, where_row,
-    slope_one, slope_two, kept_a, kept_b, kept_c, pick, place, place_far, slots,
+    flip, rest, tangent, codes, near, courant, background, w_first, w_second, where_col, where_row, slots,
+    slope_one, slope_two, kept_a, kept_b, kept_c, pick, place, place_far, near_codes,
     table, mats, cells_b, mid_b, mid_f, hidden,
 ):
     rows, lon = tangent.shape[0], tangent.shape[1]
     cells = rows * lon
     sign = sign_of(flip)
     table[...] = jnp.zeros_like(table)
-    store_sources(table, 1, own[cells:, 0:lon], False, sign, lon, rows)
-    store_sources(table, 2, near[cells:, 0:lon], True, sign, lon, rows)
+    near_codes[...] = near[cells:, 0:lon].astype(F32)
+    store_sources(table, 1, codes[...], False, sign, lon, rows)
+    store_sources(table, 2, near_codes[...], True, sign, lon, rows)
     turned = table[...].T
     k = 0
     for step, exts in enumerate(((5, 7, 9), (6, 8), (7,))):
         for ext in exts:
             pull_matrix(mats.at[k], turned, step, ext, lon, rows)
             k += 1
-    cells_b[0:cells, :] = own[0:cells, :]
     for j in range(rows):
+        row = tangent[jnp.where(flip[0] == 1, rows - 1 - j, j)]
+        cells_b[j * lon : (j + 1) * lon, :] = row.astype(BF16)
         cells_b[(rows + j) * lon : (rows + j + 1) * lon, :] = near[(rows - 1 - j) * lon : (rows - j) * lon, :]
 
     def start_f(at, size):
@@ -288,24 +302,23 @@
     place[...] = jnp.where(
         where_row[...] == lax.broadcasted_iota(jnp.int32, (cells, count), 0), 1.0, 0.0
     ).astype(BF16)
-    where, _ = slot_of(cells_reached(wind_fields(own[cells:, 0:lon], sign, rows), rows))
-    slots[...] = where
-    place_far[...] = dot(choose_matrix(where, place_far.shape[0], rows), place[...]).astype(BF16)
+    place_far[...] = dot(choose_matrix(slots[...], place_far.shape[0], rows), place[...]).astype(BF16)
 
 
 def observe_kernel(
-    flip, flag, tangent, own, far, rest, courant, slope_one, slope_two, kept_a, kept_b, kept_c,
+    flip, flag, tangent, codes, far, rest, courant, slope_one, slope_two, kept_a, kept_b, kept_c,
     w_first, w_second, w_third, pick, place, place_far, quality, chan_weight,
-    out, sent,
+    out, sent, far_codes,
     table, mats, cells_b, mid_b, mid_f, last_b, one_b, two_b, rest_b, sem,
 ):
     rows, lon = tangent.shape[0], tangent.shape[1]
     cells = rows * lon
     sign = sign_of(flip)
-    capacity = far.shape[0] - (own.shape[0] - cells)
+    capacity = far.shape[0] - codes.shape[0]
     table[...] = jnp.zeros_like(table)
-    store_sources(table, 0, far[capacity:, 0:lon], True, sign, lon, rows)
-    store_sources(table, 1, own[cells:, 0:lon], False, sign, lon, rows)
+    far_codes[...] = far[capacity:, 0:lon].astype(F32)
+    store_sources(table, 0, far_codes[...], True, sign, lon, rows)
+    store_sources(table, 1, codes[...], False, sign, lon, rows)
     turned = table[...].T
     for step in range(4):
         for half in range(2):
@@ -315,7 +328,9 @@
     for j in range(rows):
         value = dot(spread_matrix(where, j, capacity), far[0:capacity, :])
         cells_b[(rows - 1 - j) * lon : (rows - j) * lon, :] = value.astype(BF16)
-    cells_b[cells:, :] = own[0 : 2 * lon, :]
+    for j in range(2):
+        row = tangent[jnp.where(flip[0] == 1, rows - 1 - j, j)]
+        cells_b[(rows + j) * lon : (rows + j + 1) * lon, :] = row.astype(BF16)
 
     @pl.when(flag[0] > 0)
     def _():
@@ -356,18 +371,16 @@
 
 
 def near_adjoint_kernel(
-    flip, cells_own, cells_near, own, near, far, own_slots, courant,
-    kept_a, kept_b, kept_c, far_mats, spread, far_slots, over,
+    flip, rest, cells_own, cells_near, codes, near_codes, far_codes, courant,
+    kept_a, kept_b, kept_c, far_mats, spread, far_slots,
     table, mats, cells_b, mid_b, mid_f,
 ):
     rows, lon = 4, table.shape[1]
     cells = rows * lon
     sign = sign_of(flip)
-    head = own.shape[0] - cells
-    far_codes = far[far.shape[0] - head :, 0:lon]
-    store_sources(table, 0, far_codes, True, sign, lon, rows)
-    store_sources(table, 1, own[cells:, 0:lon], False, sign, lon, rows)
-    store_sources(table, 2, near[cells:, 0:lon], True, sign, lon, rows)
+    store_sources(table, 0, far_codes[...], True, sign, lon, rows)
+    store_sources(table, 1, codes[...], False, sign, lon, rows)
+    store_sources(table, 2, near_codes[...], True, sign, lon, rows)
     k = 0
     for order, exts in enumerate(((5, 7, 9), (6, 8), (7,))):
         for ext in exts:
@@ -386,14 +399,12 @@
     for order in range(4):
         for half in range(2):
             push_matrix(far_mats.at[2 * order + half], table, 3 - order, order + 1 + 2 * half, lon, rows)
-    where, total = slot_of(cells_reached(wind_fields(far_codes, -sign, rows), rows))
+    where, _ = slot_of(cells_reached(wind_fields(far_codes[...], -sign, rows), rows))
     far_slots[...] = where
     where = turn(where)
     capacity = spread.shape[1]
     for j in range(rows):
         spread[j * lon : (j + 1) * lon, :] = spread_matrix(where, j, capacity)
-    most = jnp.maximum(jnp.max(own_slots[...], axis=(0, 1), keepdims=True) + 1.0, total)
-    over[...] = jnp.broadcast_to(jnp.where(most > float(capacity), 1.0, 0.0), over.shape)
 
 
 def far_adjoint_kernel(
@@ -455,7 +466,6 @@
             out_shape=out,
             in_specs=[VMEM, VMEM],
             out_specs=VMEM,
-            compiler_params=params(),
             name="rest",
         )(slots, dense)
         return lax.ppermute(rest, "lat", links)
@@ -493,27 +503,39 @@
     links = [(i, i + 1) for i in range(1, count - 1, 2)]
     links = links + [(b, a) for a, b in links]
 
-    own, sent, slots, over = pl.pallas_call(
+    own, sent, codes, slots = pl.pallas_call(
         pack_kernel,
         out_shape=[
             shape((cells + head, levels), BF16),
             shape((FAR_CELLS + head, levels), BF16),
+            shape((head, lon), F32),
             shape((8, lon), F32),
-            shape((8, lon), F32),
-        ],
-        in_specs=[SMEM, HBM, VMEM],
+        ],
+        in_specs=[SMEM, HBM, HBM],
         out_specs=[VMEM] * 4,
         scratch_shapes=[
             pltpu.VMEM((rows, lon, levels), F32),
-            pltpu.VMEM((head, lon), F32),
-            pltpu.SemaphoreType.DMA((rows,)),
-        ],
-        compiler_params=params(),
+            pltpu.VMEM(wind_code.shape, jnp.int32),
+            pltpu.SemaphoreType.DMA((rows + 1,)),
+        ],
+        compiler_params=pltpu.CompilerParams(vmem_limit_bytes=PACK_LIMIT),
         name="pack",
     )(flip, tangent, wind_code)
 
     far = lax.ppermute(sent, "lat", links)
     near = lax.ppermute(own, "lat", pairs)
+
+    own_slots, over = pl.pallas_call(
+        reach_kernel,
+        out_shape=[shape((8, lon), F32)] * 2,
+        in_specs=[SMEM, ANY, VMEM, VMEM],
+        out_specs=[VMEM] * 2,
+        name="reach",
+    )(flip, near, codes, slots)
+    over = jnp.maximum(over, lax.ppermute(over, "lat", links))
+    first_over = linked & (over[0, 0] > 0.0)
+    second_over = linked & (over[0, 1] > 0.0)
+    rest = second_exchange(first_over, FAR_CELLS, slots, own, cells - FAR_CELLS, links)
 
     c_row = courant.reshape(1, levels)
     slot_ids = jnp.arange(listed, dtype=jnp.int32)
@@ -525,7 +547,7 @@
 
     kept_shape = [shape((2 * lon, levels), F32)] * 3
     slope_shape = shape((listed, hidden_size), F32)
-    slope_one, slope_two, kept_a, kept_b, kept_c, pick, place, place_far, own_slots = pl.pallas_call(
+    slope_one, slope_two, kept_a, kept_b, kept_c, pick, place, place_far, near_codes = pl.pallas_call(
         near_kernel,
         out_shape=[slope_shape, slope_shape]
         + kept_shape
@@ -533,9 +555,9 @@
             shape((listed, cells), BF16),
             shape((cells, listed), BF16),
             shape((FAR_COLUMNS, listed), BF16),
-            shape((8, lon), F32),
-        ],
-        in_specs=[SMEM] + [VMEM] * 9,
+            shape((head, lon), F32),
+        ],
+        in_specs=[SMEM, ANY] + [VMEM] * 10,
         out_specs=[VMEM] * 9,
         scratch_shapes=[
             pltpu.VMEM((lon, lon), F32),
@@ -549,17 +571,19 @@
         cost_estimate=pl.CostEstimate(flops=4_000_000_000, bytes_accessed=16_000_000, transcendentals=1_000_000),
         name="near",
     )(
-        flip, tangent, own, near, c_row, background[0], w_first, w_second,
-        where_at.reshape(listed, 1), where_at.reshape(1, listed),
-    )
-
-    flag = linked & ((over[0, 0] > 0.0) | (far[FAR_CELLS, 2 * lon] > 0.0))
-    rest = second_exchange(flag, FAR_CELLS, slots, own, cells - FAR_CELLS, links)
-    cells_own, sent = pl.pallas_call(
+        flip, rest, tangent, codes, near, c_row, background[0], w_first, w_second,
+        where_at.reshape(listed, 1), where_at.reshape(1, listed), own_slots,
+    )
+
+    cells_own, sent, far_codes = pl.pallas_call(
         observe_kernel,
-        out_shape=[shape((cells, levels), BF16), shape((FAR_COLUMNS, levels), BF16)],
+        out_shape=[
+            shape((cells, levels), BF16),
+            shape((FAR_COLUMNS, levels), BF16),
+            shape((head, lon), F32),
+        ],
         in_specs=[SMEM, SMEM, VMEM, VMEM, VMEM, ANY] + [VMEM] * 14,
-        out_specs=[VMEM] * 2,
+        out_specs=[VMEM] * 3,
         scratch_shapes=[
             pltpu.VMEM((lon, lon), F32),
             pltpu.VMEM((8, 2 * lon, 4 * lon), BF16),
@@ -575,7 +599,7 @@
         compiler_params=params(),
         name="observe",
     )(
-        flip, flag.astype(jnp.int32).reshape(1), tangent, own, far, rest, c_row,
+        flip, first_over.astype(jnp.int32).reshape(1), tangent, codes, far, rest, c_row,
         slope_one, slope_two, kept_a, kept_b, kept_c, w_first, w_second, w_third,
         pick, place, place_far, quality.reshape(listed, 1), chan_weight.reshape(1, -1),
     )
@@ -583,17 +607,17 @@
     columns_far = lax.ppermute(sent, "lat", links)
     cells_near = lax.ppermute(cells_own, "lat", pairs)
 
-    kept_a, kept_b, kept_c, mats, spread, far_slots, over = pl.pallas_call(
+    rest = second_exchange(second_over, FAR_COLUMNS, own_slots, cells_own, cells - FAR_COLUMNS, links)
+    kept_a, kept_b, kept_c, mats, spread, far_slots = pl.pallas_call(
         near_adjoint_kernel,
         out_shape=kept_shape
         + [
             shape((8, 2 * lon, 4 * lon), BF16),
             shape((cells, FAR_COLUMNS), BF16),
             shape((8, lon), F32),
-            shape((8, lon), F32),
-        ],
-        in_specs=[SMEM] + [VMEM] * 7,
-        out_specs=[VMEM] * 7,
+        ],
+        in_specs=[SMEM, ANY] + [VMEM] * 6,
+        out_specs=[VMEM] * 6,
         scratch_shapes=[
             pltpu.VMEM((lon, lon), F32),
             pltpu.VMEM((6, 2 * lon, 4 * lon), BF16),
@@ -604,10 +628,8 @@
         compiler_params=params(),
         cost_estimate=pl.CostEstimate(flops=2_000_000_000, bytes_accessed=8_000_000, transcendentals=0),
         name="near_adjoint",
-    )(flip, cells_own, cells_near, own, near, far, own_slots, c_row)
-
-    flag = linked & (over[0, 0] > 0.0)
-    rest = second_exchange(flag, FAR_COLUMNS, own_slots, cells_own, cells - FAR_COLUMNS, links)
+    )(flip, rest, cells_own, cells_near, codes, near_codes, far_codes, c_row)
+
     return pl.pallas_call(
         far_adjoint_kernel,
         out_shape=shape((rows, lon, levels), F32),
@@ -624,7 +646,7 @@
         compiler_params=params(),
         name="far_adjoint",
     )(
-        flip, flag.astype(jnp.int32).reshape(1), cells_own, columns_far, rest, c_row,
+        flip, second_over.astype(jnp.int32).reshape(1), cells_own, columns_far, rest, c_row,
         kept_a, kept_b, kept_c, mats, spread, far_slots,
     )
 

time: 76.1 us -> 73.5 us (0.966)
  local copies, waits for them, and re-layouts: 14.2 us -> 9.91 us
  waiting for transfers between devices: 19.5 us -> 15.5 us
  other arithmetic: 0.26 us -> 3.67 us
  starting transfers between devices: 5.91 us -> 8.27 us
    ppermute x1, waiting for transfers between devices: 13.4 us -> 0.01 us  [local(): far = lax.ppermute(sent, 'lat', links)]
    ppermute x0 -> x1, waiting for transfers between devices: none -> 5.59 us  [local(): over = jnp.maximum(over, lax.ppermute(over, 'lat', links))]
    unnamed x36 -> x26, local copies, waits for them, and re-layouts: 12.2 us -> 7.58 us
    ppermute x1, waiting for transfers between devices: 5.39 us -> 9.66 us  [local(): columns_far = lax.ppermute(sent, 'lat', links)]
    ppermute x0 -> x1, starting transfers between devices: none -> 2.49 us  [local(): over = jnp.maximum(over, lax.ppermute(over, 'lat', links))]
    pallas_call x1, Pallas kernels: 6.32 us -> 4.43 us  [local(): pl.pallas_call(near_kernel, out_shape=[slope_shape, slope_shape] + kept_s...]
    pallas_call x0 -> x1, Pallas kernels: none -> 1.75 us  [local(): pl.pallas_call(reach_kernel, out_shape=[shape((8, lon), F32)] * 2, in_spe...]
    select_n x2, other arithmetic: 0.23 us -> 1.87 us  [local(): where_at = jnp.where(observed, where_at, -1)]
  transfers between devices with their start and end apart: 4 -> 5, of which waited for: 3 -> 3; matrix products, arithmetic and copies ran while one was open for 3% -> 8% of each run, Pallas kernels for 6% -> 14%
where the time goes in v2:
time: 73.5 us; the launch traced here: 72.9 us
  Pallas kernels  33.2 us (45%)
  waiting for transfers between devices  15.5 us (21%)
  local copies, waits for them, and re-layouts  9.91 us (13%)
  starting transfers between devices  8.27 us (11%)
  other arithmetic  3.67 us (5%)
  between operations  2.32 us (3%)
    pallas_call x1, Pallas kernels, local(): pl.pallas_call(observe_kernel, out_shape=[shape((cells, levels), BF16), s...  13.8 us
    ppermute x1, waiting for transfers between devices, local(): columns_far = lax.ppermute(sent, 'lat', links)  9.66 us
    unnamed x26, local copies, waits for them, and re-layouts  7.58 us
    pallas_call x1, Pallas kernels, local(): pl.pallas_call(far_adjoint_kernel, out_shape=shape((rows, lon, levels), F...  5.91 us
    ppermute x1, waiting for transfers between devices, local(): over = jnp.maximum(over, lax.ppermute(over, 'lat', links))  5.59 us
    pallas_call x1, Pallas kernels, local(): pl.pallas_call(near_kernel, out_shape=[slope_shape, slope_shape] + kept_s...  4.43 us
    pallas_call x1, Pallas kernels, local(): pl.pallas_call(near_adjoint_kernel, out_shape=kept_shape + [shape((8, 2 *...  4.29 us
    ppermute x1, starting transfers between devices, local(): far = lax.ppermute(sent, 'lat', links)  3.05 us
  transfers between devices with their start and end apart: 5, of which 3 were waited for; matrix products, arithmetic and copies ran while one was open for 8% of the time, Pallas kernels for 14%

profile of v2, /device:TPU:25, one launch (start us, length us, event | category | flops | bytes accessed | tf_op | source)
XLA Modules:
  0.0 72.9 jit_solution(5746512941068388053)
XLA Ops:
  0.0 0.0 copy-start.12
  0.0 0.0 copy-start.11
  0.0 3.0 %pack.1 = (bf16[528,1024]{1,0:T(8,128)(2,1)}, bf16[320,1024]{1,0:T(8,128)(2,1)}, f32[16,128]{1,0:T(8,128)}, f32[8,128]{1,0:T(8,128)S(1)}) custom-call(s32[1]{0:T(128)} %bitcast.flip, f32[4,128,1024]{2,1,0:T(8,128)} %tangent.5, s32[4,4,128]{2,1,0:T(4,128)} %wind.1), custom_call_target="tpu_custom_call" | custom-call | tf_op jit(solution)/shard_map/pack/pallas_call | solution.py:506
  3.0 0.7 %collective-permute-start.2 = (bf16[528,1024]{1,0:T(8,128)(2,1)}, bf16[528,1024]{1,0:T(8,128)(2,1)S(1)}, u32[]{:S(2)}, u32[]{:S(2)}) collective-permute-start(bf16[528,1024]{1,0:T(8,128)(2,1)} %get-tuple-element.47), channel_id=1, source_target_pairs={{0,1},{1,0},{2,3},{3,2},{4,5},{5,4},{6,7},{7,6},{8,9},{9,8},{10,11... | collective-permute-start | bytes 3244040 | tf_op jit(solution)/shard_map/ppermute | solution.py:526
  3.8 3.0 %collective-permute-start.4 = (bf16[320,1024]{1,0:T(8,128)(2,1)}, bf16[320,1024]{1,0:T(8,128)(2,1)}, u32[]{:S(2)}, u32[]{:S(2)}) collective-permute-start(bf16[320,1024]{1,0:T(8,128)(2,1)} %get-tuple-element.51), channel_id=1, source_target_pairs={{1,2},{3,4},{5,6},{7,8},{9,10},{11,12},{13,14},{2,1},{4,3},{6,5},{... | collective-permute-start | bytes 1966088 | tf_op jit(solution)/shard_map/ppermute | solution.py:525
  7.5 0.0 copy-done.12
  7.5 0.9 %copy.18 = f32[480,1]{1,0:T(8,128)} copy(f32[480,1]{0,1:T(1,128)S(1)} %bitcast_convert_fusion) | data formatting | bytes 3840 | tf_op jit(solution)/shard_map/convert_element_type | solution.py:546
  8.4 0.0 copy-done.11
  8.4 0.8 %copy.16 = s32[480,1]{1,0:T(8,128)} copy(s32[480,1]{0,1:T(1,128)S(1)} %bitcast.22) | data formatting | bytes 3840 | tf_op jit(solution)/shard_map/squeeze | solution.py:543
  9.2 0.0 copy-start
  9.2 0.0 copy-start.7
  9.2 0.0 copy-start.8
  9.2 1.1 %fusion.5.quality = f32[480,1]{1,0:T(8,128)S(1)} fusion(f32[480,1]{1,0:T(8,128)} %copy.18, s32[]{:T(128)} %bitcast.15), kind=kLoop, calls=%fused_computation.12 | loop fusion | flops 960 | bytes 3844 | tf_op jit(solution)/shard_map/jit(_where)/select_n | solution.py:546
  10.3 1.8 %fusion.4.where_col = s32[480,1]{1,0:T(8,128)} fusion(s32[480,1]{1,0:T(8,128)} %copy.16, s32[]{:T(128)} %bitcast.13, pred[]{:T(512)S(6)} %eq.5), kind=kLoop, calls=%fused_computation.9 | loop fusion | flops 10560 | bytes 3845 | tf_op jit(solution)/shard_map/jit(_where)/select_n | solution.py:545
  12.2 0.0 collective-permute-done.2.after.near
  12.2 0.0 copy-start.4
  12.2 1.0 %copy-done.4 = bf16[528,1024]{1,0:T(8,128)(2,1)} copy-done((bf16[528,1024]{1,0:T(8,128)(2,1)}, bf16[528,1024]{1,0:T(8,128)(2,1)S(1)}, u32[]{:S(2)}) %copy-start.4) | copy-done | bytes 1081368
  13.2 1.8 %reach.1 = (f32[8,128]{1,0:T(8,128)S(1)}, f32[8,128]{1,0:T(8,128)}) custom-call(s32[1]{0:T(128)} %bitcast.flip, bf16[528,1024]{1,0:T(8,128)(2,1)} %copy-done.4, f32[16,128]{1,0:T(8,128)} %get-tuple-element.48.codes, f32[8,128]{1,0:T(8,128)S(1)} %get-tuple-element.49.pulled_slots), custom_call_target="tpu_custom_call" | custom-call | tf_op jit(solution)/shard_map/reach/pallas_call | solution.py:528
  14.9 2.5 %collective-permute-start.3 = (f32[8,128]{1,0:T(8,128)}, f32[8,128]{1,0:T(8,128)S(1)}, u32[]{:S(2)}, u32[]{:S(2)}) collective-permute-start(f32[8,128]{1,0:T(8,128)} %get-tuple-element.50), channel_id=1, source_target_pairs={{1,2},{3,4},{5,6},{7,8},{9,10},{11,12},{13,14},{2,1},{4,3},{6,5},{... | collective-permute-start | bytes 12296 | tf_op jit(solution)/shard_map/ppermute | solution.py:535
  17.5 5.6 %collective-permute-done.3 = f32[8,128]{1,0:T(8,128)S(1)} collective-permute-done((f32[8,128]{1,0:T(8,128)}, f32[8,128]{1,0:T(8,128)S(1)}, u32[]{:S(2)}, u32[]{:S(2)}) %collective-permute-start.3) | collective-permute-done | bytes 4128 | tf_op jit(solution)/shard_map/ppermute | solution.py:535
  23.1 0.7 max.3
  23.7 0.6 fusion.7
  25.1 0.0 copy-done
  25.1 0.0 copy-done.7
  25.1 0.0 copy-done.8
  25.1 0.0 copy-start.1
  25.1 1.6 %copy-done.1 = bf16[1024,1024]{1,0:T(8,128)(2,1)S(1)} copy-done((bf16[1024,1024]{1,0:T(8,128)(2,1)S(1)}, bf16[1024,1024]{1,0:T(8,128)(2,1)}, u32[]{:S(2)}) %copy-start.1) | copy-done | bytes 2097176
  26.7 0.0 copy-start.2
  26.7 1.6 %copy-done.2 = bf16[1024,1024]{1,0:T(8,128)(2,1)S(1)} copy-done((bf16[1024,1024]{1,0:T(8,128)(2,1)S(1)}, bf16[1024,1024]{1,0:T(8,128)(2,1)}, u32[]{:S(2)}) %copy-start.2) | copy-done | bytes 2097176
  28.3 0.0 copy-start.5
  28.3 1.2 %copy-done.5 = bf16[528,1024]{1,0:T(8,128)(2,1)S(1)} copy-done((bf16[528,1024]{1,0:T(8,128)(2,1)S(1)}, bf16[528,1024]{1,0:T(8,128)(2,1)}, u32[]{:S(2)}) %copy-start.5) | copy-done | bytes 1081368
  29.5 0.0 copy-start.6
  29.5 0.9 %copy-done.6 = s32[480,1]{1,0:T(8,128)S(1)} copy-done((s32[480,1]{1,0:T(8,128)S(1)}, s32[480,1]{1,0:T(8,128)}, u32[]{:S(2)}) %copy-start.6) | copy-done | bytes 1944
  30.5 0.0 copy-start.10
  30.5 1.2 %copy-done.10 = bf16[1,480,1024]{2,1,0:T(8,128)(2,1)S(1)} copy-done((bf16[1,480,1024]{2,1,0:T(8,128)(2,1)S(1)}, bf16[1,480,1024]{2,1,0:T(8,128)(2,1)}, u32[]{:S(2)}) %copy-start.10) | copy-done | bytes 983064
  31.7 0.0 copy-start.3
  31.7 0.0 copy-start.9
  31.7 4.4 %near.1 = (f32[480,1024]{1,0:T(8,128)S(1)}, f32[480,1024]{1,0:T(8,128)S(1)}, f32[256,1024]{1,0:T(8,128)S(1)}, f32[256,1024]{1,0:T(8,128)S(1)}, f32[256,1024]{1,0...) custom-call(s32[1]{0:T(128)} %bitcast.flip, ...), custom_call_target="tpu_custom_call" | custom-call | flops 4000000000 | bytes 16000000 | tf_op jit(solution)/shard_map/near/pallas_call | solution.py:550
  36.1 0.0 collective-permute-done.4.far
  36.1 0.0 copy-done.3
  36.1 0.0 copy-done.9
  36.2 13.8 %observe.1 = (bf16[512,1024]{1,0:T(8,128)(2,1)}, bf16[272,1024]{1,0:T(8,128)(2,1)S(1)}, f32[16,128]{1,0:T(8,128)S(1)}) custom-call(s32[1]{0:T(128)} %bitcast.flip, s32[1]{0:T(128)} %bitcast.4.flag, f32[4,128,1024]{2,1,0:T(8,128)S(1)} %copy-done, f32[16,128]{1,0:T(8,128)S(1)} %copy-done.7, bf16[320,1024]{1,0:T(8,128)(2,1)} %collective-permute-done.4.far, ...), custom_call_target="tpu_custom_call" | custom-call | tf_op jit(solution)/shard_map/observe/pallas_call | solution.py:578
  49.9 0.1 collective-permute-start.6
  50.0 1.9 %collective-permute-start.5 = (bf16[272,1024]{1,0:T(8,128)(2,1)S(1)}, bf16[272,1024]{1,0:T(8,128)(2,1)S(1)}, u32[]{:S(2)}, u32[]{:S(2)}) collective-permute-start(bf16[272,1024]{1,0:T(8,128)(2,1)S(1)} %get-tuple-element.62), channel_id=1, source_target_pairs={{1,2},{3,4},{5,6},{7,8},{9,10},{11,12},{13,14},{2,1},{4,3},{6,5},{... | collective-permute-start | bytes 1671176 | tf_op jit(solution)/shard_map/ppermute | solution.py:607
  52.6 0.3 collective-permute-done.6.cells_near
  52.9 4.3 %near_adjoint.1 = (f32[256,1024]{1,0:T(8,128)S(1)}, f32[256,1024]{1,0:T(8,128)S(1)}, f32[256,1024]{1,0:T(8,128)S(1)}, bf16[8,256,512]{2,1,0:T(8,128)(2,1)S(1)}, ...) custom-call(s32[1]{0:T(128)} %bitcast.flip, bf16[240,1024]{1,0:T(8,128)(2,1)} %get-tuple-element.74.rest, ...), custom_call_target="tpu_custom_call" | custom-call | flops 2000000000 | bytes 8000000 | tf_op jit(solution)/shard_map/near_adjoint/pallas_call | solution.py:611
  57.2 9.7 %collective-permute-done.5.far = bf16[272,1024]{1,0:T(8,128)(2,1)S(1)} collective-permute-done((bf16[272,1024]{1,0:T(8,128)(2,1)S(1)}, bf16[272,1024]{1,0:T(8,128)(2,1)S(1)}, u32[]{:S(2)}, u32[]{:S(2)}) %collective-permute-start.5) | collective-permute-done | bytes 557088 | tf_op jit(solution)/shard_map/ppermute | solution.py:607
  66.8 5.9 %far_adjoint.1 = f32[4,128,1024]{2,1,0:T(8,128)} custom-call(s32[1]{0:T(128)} %bitcast.flip, s32[1]{0:T(128)} %bitcast.2.flag, bf16[512,1024]{1,0:T(8,128)(2,1)} %get-tuple-element.61.cells_own, bf16[272,1024]{1,0:T(8,128)(2,1)S(1)} %collective-permute-done.5.far, bf16[240,1024]{1,0:T(8,128)(2,1)} %get-tuple-element.74.rest, f32[1,1024]{1,0:T(1,128)S(1)} %bitcast.19, ...), custom_call_target="tpu_custom_call" | custom-call | tf_op jit(solution)/shard_map/far_adjoint/pallas_call | solution.py:633
  (6 shorter events, 0.1 us)
Async XLA Ops:
  0.0 7.5 %copy-start.12 = (bf16[1,480]{1,0:T(2,128)(2,1)S(1)}, bf16[1,480]{1,0:T(2,128)(2,1)}, u32[]{:S(2)}) copy-start(bf16[1,480]{1,0:T(2,128)(2,1)} %param.20) | copy-start | bytes 2884
  0.0 8.4 %copy-start.11 = (s32[1,480]{1,0:T(1,128)S(1)}, s32[1,480]{1,0:T(1,128)}, u32[]{:S(2)}) copy-start(s32[1,480]{1,0:T(1,128)} %param.18) | copy-start | bytes 5764
  3.0 9.1 %collective-permute-start.2 = (bf16[528,1024]{1,0:T(8,128)(2,1)}, bf16[528,1024]{1,0:T(8,128)(2,1)S(1)}, u32[]{:S(2)}, u32[]{:S(2)}) collective-permute-start(bf16[528,1024]{1,0:T(8,128)(2,1)} %get-tuple-element.47), channel_id=1, source_target_pairs={{0,1},{1,0},{2,3},{3,2},{4,5},{5,4},{6,7},{7,6},{8,9},{9,8},{10,11... | collective-permute-start | bytes 3244040 | tf_op jit(solution)/shard_map/ppermute | solution.py:526
  3.8 32.3 %collective-permute-start.4 = (bf16[320,1024]{1,0:T(8,128)(2,1)}, bf16[320,1024]{1,0:T(8,128)(2,1)}, u32[]{:S(2)}, u32[]{:S(2)}) collective-permute-start(bf16[320,1024]{1,0:T(8,128)(2,1)} %get-tuple-element.51), channel_id=1, source_target_pairs={{1,2},{3,4},{5,6},{7,8},{9,10},{11,12},{13,14},{2,1},{4,3},{6,5},{... | collective-permute-start | bytes 1966088 | tf_op jit(solution)/shard_map/ppermute | solution.py:525
  9.2 15.9 %copy-start = (f32[4,128,1024]{2,1,0:T(8,128)S(1)}, f32[4,128,1024]{2,1,0:T(8,128)}, u32[]{:S(2)}) copy-start(f32[4,128,1024]{2,1,0:T(8,128)} %tangent.5) | copy-start | bytes 6291460
  9.2 15.9 %copy-start.7 = (f32[16,128]{1,0:T(8,128)S(1)}, f32[16,128]{1,0:T(8,128)}, u32[]{:S(2)}) copy-start(f32[16,128]{1,0:T(8,128)} %get-tuple-element.48.codes) | copy-start | bytes 24580
  9.2 15.9 %copy-start.8 = (f32[1024]{0:T(1024)S(1)}, f32[1024]{0:T(1024)}, u32[]{:S(2)}) copy-start(f32[1024]{0:T(1024)} %param.17) | copy-start | bytes 12292
  12.2 1.0 %copy-start.4 = (bf16[528,1024]{1,0:T(8,128)(2,1)}, bf16[528,1024]{1,0:T(8,128)(2,1)S(1)}, u32[]{:S(2)}) copy-start(bf16[528,1024]{1,0:T(8,128)(2,1)S(1)} %collective-permute-done.2.after.near) | copy-start | bytes 3244036
  14.9 8.1 %collective-permute-start.3 = (f32[8,128]{1,0:T(8,128)}, f32[8,128]{1,0:T(8,128)S(1)}, u32[]{:S(2)}, u32[]{:S(2)}) collective-permute-start(f32[8,128]{1,0:T(8,128)} %get-tuple-element.50), channel_id=1, source_target_pairs={{1,2},{3,4},{5,6},{7,8},{9,10},{11,12},{13,14},{2,1},{4,3},{6,5},{... | collective-permute-start | bytes 12296 | tf_op jit(solution)/shard_map/ppermute | solution.py:535
  25.1 1.6 %copy-start.1 = (bf16[1024,1024]{1,0:T(8,128)(2,1)S(1)}, bf16[1024,1024]{1,0:T(8,128)(2,1)}, u32[]{:S(2)}) copy-start(bf16[1024,1024]{1,0:T(8,128)(2,1)} %w_first.3) | copy-start | bytes 6291460
  26.7 1.6 %copy-start.2 = (bf16[1024,1024]{1,0:T(8,128)(2,1)S(1)}, bf16[1024,1024]{1,0:T(8,128)(2,1)}, u32[]{:S(2)}) copy-start(bf16[1024,1024]{1,0:T(8,128)(2,1)} %w_second.3) | copy-start | bytes 6291460
  28.3 1.2 %copy-start.5 = (bf16[528,1024]{1,0:T(8,128)(2,1)S(1)}, bf16[528,1024]{1,0:T(8,128)(2,1)}, u32[]{:S(2)}) copy-start(bf16[528,1024]{1,0:T(8,128)(2,1)} %copy-done.4) | copy-start | bytes 3244036
  29.5 0.9 %copy-start.6 = (s32[480,1]{1,0:T(8,128)S(1)}, s32[480,1]{1,0:T(8,128)}, u32[]{:S(2)}) copy-start(s32[480,1]{1,0:T(8,128)} %fusion.4.where_col) | copy-start | bytes 5764
  30.5 1.2 %copy-start.10 = (bf16[1,480,1024]{2,1,0:T(8,128)(2,1)S(1)}, bf16[1,480,1024]{2,1,0:T(8,128)(2,1)}, u32[]{:S(2)}) copy-start(bf16[1,480,1024]{2,1,0:T(8,128)(2,1)} %param.21) | copy-start | bytes 2949124
  31.7 4.5 %copy-start.3 = (bf16[1024,1024]{1,0:T(8,128)(2,1)S(1)}, bf16[1024,1024]{1,0:T(8,128)(2,1)}, u32[]{:S(2)}) copy-start(bf16[1024,1024]{1,0:T(8,128)(2,1)} %w_third.1) | copy-start | bytes 6291460
  31.7 4.5 %copy-start.9 = (f32[1024]{0:T(1024)S(1)}, f32[1024]{0:T(1024)}, u32[]{:S(2)}) copy-start(f32[1024]{0:T(1024)} %param.25) | copy-start | bytes 12292
  49.9 2.9 %collective-permute-start.6 = (bf16[512,1024]{1,0:T(8,128)(2,1)}, bf16[512,1024]{1,0:T(8,128)(2,1)S(1)}, u32[]{:S(2)}, u32[]{:S(2)}) collective-permute-start(bf16[512,1024]{1,0:T(8,128)(2,1)} %get-tuple-element.61.cells_own), channel_id=1, source_target_pairs={{0,1},{1,0},{2,3},{3,2},{4,5},{5,4},{6,7},{7,6},{8,9},{9,8},{10,11... | collective-permute-start | bytes 3145736 | tf_op jit(solution)/shard_map/ppermute | solution.py:608
  50.0 16.8 %collective-permute-start.5 = (bf16[272,1024]{1,0:T(8,128)(2,1)S(1)}, bf16[272,1024]{1,0:T(8,128)(2,1)S(1)}, u32[]{:S(2)}, u32[]{:S(2)}) collective-permute-start(bf16[272,1024]{1,0:T(8,128)(2,1)S(1)} %get-tuple-element.62), channel_id=1, source_target_pairs={{1,2},{3,4},{5,6},{7,8},{9,10},{11,12},{13,14},{2,1},{4,3},{6,5},{... | collective-permute-start | bytes 1671176 | tf_op jit(solution)/shard_map/ppermute | solution.py:607

commit v3 on v2

--- a/solution.py
+++ b/solution.py
@@ -167,12 +167,13 @@
             code = jnp.where(flip[0] == 1, wind_b[step, rows - 1 - j : rows - j, :], wind_b[step, j : j + 1, :])
             codes[step * rows + j : step * rows + j + 1, :] = code.astype(F32) + 1.0
     mask = cells_pulled(wind_fields(codes[...], sign_of(flip), rows), rows)
-    where, _ = slot_of(mask)
+    where, total = slot_of(mask)
     slots[...] = where
     head = codes.shape[0]
     capacity = sent.shape[0] - head
     tall = jnp.concatenate([mask, jnp.zeros((head - mask.shape[0], lon), F32)], axis=0)
-    notes = jnp.concatenate([codes[...], tall, jnp.zeros((head, own.shape[1] - 2 * lon), F32)], axis=1)
+    flag = jnp.broadcast_to(jnp.where(total > float(capacity), 1.0, 0.0), (head, lon))
+    notes = jnp.concatenate([codes[...], tall, flag, jnp.zeros((head, own.shape[1] - 3 * lon), F32)], axis=1)
     notes = notes.astype(BF16)
     own[cells:, :] = notes
     sent[capacity:, :] = notes
@@ -183,15 +184,24 @@
     sent[0:capacity, :] = dot(choose, own[0:cells, :]).astype(BF16)
 
 
-def reach_kernel(flip, after, codes, pulled_slots, slots, over):
-    rows = 4
-    where, total = slot_of(cells_reached(wind_fields(codes[...], sign_of(flip), rows), rows))
-    slots[...] = where
-    pulled = jnp.max(pulled_slots[...], axis=(0, 1), keepdims=True) + 1.0
-    line = lax.broadcasted_iota(jnp.int32, over.shape, 1)
-    first = jnp.where(pulled > float(FAR_CELLS), 1.0, 0.0)
-    second = jnp.where(total > float(FAR_COLUMNS), 1.0, 0.0)
-    over[...] = jnp.where(line == 0, first, jnp.where(line == 1, second, 0.0))
+def reach_kernel(flip, linked, own_slots, far_codes, far_slots, over):
+    where, total = slot_of(cells_reached(wind_fields(far_codes[...], -sign_of(flip), 4), 4))
+    far_slots[...] = where
+    most = jnp.maximum(total, jnp.max(own_slots[...], axis=(0, 1), keepdims=True) + 1.0)
+    over[0] = jnp.where(jnp.max(most) > float(FAR_COLUMNS), linked[0], 0)
+
+
+def choose_kernel(flag, _one, _two, redone_one, redone_two, one, two, sem):
+    @pl.when(flag[0] > 0)
+    def _():
+        copies = [
+            pltpu.make_async_copy(redone_one, one, sem.at[0]),
+            pltpu.make_async_copy(redone_two, two, sem.at[1]),
+        ]
+        for copy in copies:
+            copy.start()
+        for copy in copies:
+            copy.wait()
 
 
 def rest_kernel(first, slots, dense, out):
@@ -201,7 +211,7 @@
     out[...] = dot(choose, dense[0:cells, :]).astype(BF16)
 
 
-def blank_kernel(out):
+def blank_kernel(*outs):
     pass
 
 
@@ -253,8 +263,8 @@
 
 
 def near_kernel(
-    flip, rest, tangent, codes, near, courant, background, w_first, w_second, where_col, where_row, slots,
-    slope_one, slope_two, kept_a, kept_b, kept_c, pick, place, place_far, near_codes,
+    flip, obs_count, tangent, codes, near, courant, background, w_first, w_second, obs_index, obs_quality,
+    slope_one, slope_two, kept_a, kept_b, kept_c, pick, place, place_far, near_codes, quality, slots,
     table, mats, cells_b, mid_b, mid_f, hidden,
 ):
     rows, lon = tangent.shape[0], tangent.shape[1]
@@ -295,20 +305,28 @@
     second_tanh = jnp.tanh(dot(hidden[...], w_second[...]))
     slope_two[...] = 1.0 - second_tanh * second_tanh
 
-    count = where_col.shape[0]
-    pick[...] = jnp.where(
-        where_col[...] == lax.broadcasted_iota(jnp.int32, (count, cells), 1), 1.0, 0.0
-    ).astype(BF16)
-    place[...] = jnp.where(
-        where_row[...] == lax.broadcasted_iota(jnp.int32, (cells, count), 0), 1.0, 0.0
-    ).astype(BF16)
+    count = obs_index.shape[1]
+    at = obs_index[...]
+    at = jnp.where(flip[0] == 1, at + (rows - 1 - 2 * lax.div(at, lon)) * lon, at)
+    live = lax.broadcasted_iota(jnp.int32, at.shape, 1) < obs_count[0]
+    at = jnp.where(live, at, -1)
+    chosen = at == lax.broadcasted_iota(jnp.int32, (cells, count), 0)
+    place[...] = jnp.where(chosen, 1.0, 0.0).astype(BF16)
+    lines = jnp.concatenate([at.astype(F32), jnp.where(live, obs_quality[...].astype(F32), 0.0)], axis=0)
+    lines = jnp.concatenate([lines, jnp.zeros((6, count), F32)], axis=0)
+    lines = jnp.concatenate([lines, jnp.zeros((8, cells - count), F32)], axis=1).T
+    quality[...] = lines[0:count, 1:2]
+    columns = lax.broadcasted_iota(jnp.int32, (count, cells), 1).astype(F32)
+    pick[...] = jnp.where(lines[0:count, 0:1] == columns, 1.0, 0.0).astype(BF16)
+    where, _ = slot_of(cells_reached(wind_fields(codes[...], sign, rows), rows))
+    slots[...] = where
     place_far[...] = dot(choose_matrix(slots[...], place_far.shape[0], rows), place[...]).astype(BF16)
 
 
 def observe_kernel(
-    flip, flag, tangent, codes, far, rest, courant, slope_one, slope_two, kept_a, kept_b, kept_c,
+    redo, flip, linked, slots, tangent, codes, far, rest, courant, slope_one, slope_two, kept_a, kept_b, kept_c,
     w_first, w_second, w_third, pick, place, place_far, quality, chan_weight,
-    out, sent, far_codes,
+    out, sent, far_codes, over,
     table, mats, cells_b, mid_b, mid_f, last_b, one_b, two_b, rest_b, sem,
 ):
     rows, lon = tangent.shape[0], tangent.shape[1]
@@ -325,6 +343,8 @@
             pull_matrix(mats.at[2 * step + half], turned, step, step + 1 + 2 * half, lon, rows)
     where, _ = slot_of(far[capacity:, lon : 2 * lon].astype(F32)[0:8])
     where = turn(where)
+    most = jnp.maximum(jnp.max(far[capacity:, 2 * lon : 3 * lon].astype(F32)), jnp.where(jnp.max(slots[...]) >= float(capacity), 1.0, 0.0))
+    over[0] = jnp.where(most > 0.0, linked[0], 0)
     for j in range(rows):
         value = dot(spread_matrix(where, j, capacity), far[0:capacity, :])
         cells_b[(rows - 1 - j) * lon : (rows - j) * lon, :] = value.astype(BF16)
@@ -332,8 +352,7 @@
         row = tangent[jnp.where(flip[0] == 1, rows - 1 - j, j)]
         cells_b[(rows + j) * lon : (rows + j + 1) * lon, :] = row.astype(BF16)
 
-    @pl.when(flag[0] > 0)
-    def _():
+    if redo:
         copy = pltpu.make_async_copy(rest, rest_b, sem.at[0])
         copy.start()
         copy.wait()
@@ -371,8 +390,8 @@
 
 
 def near_adjoint_kernel(
-    flip, rest, cells_own, cells_near, codes, near_codes, far_codes, courant,
-    kept_a, kept_b, kept_c, far_mats, spread, far_slots,
+    flip, rest, cells_own, cells_near, codes, near_codes, far_codes, far_slots, courant,
+    kept_a, kept_b, kept_c, far_mats, spread,
     table, mats, cells_b, mid_b, mid_f,
 ):
     rows, lon = 4, table.shape[1]
@@ -399,9 +418,7 @@
     for order in range(4):
         for half in range(2):
             push_matrix(far_mats.at[2 * order + half], table, 3 - order, order + 1 + 2 * half, lon, rows)
-    where, _ = slot_of(cells_reached(wind_fields(far_codes[...], -sign, rows), rows))
-    far_slots[...] = where
-    where = turn(where)
+    where = turn(far_slots[...])
     capacity = spread.shape[1]
     for j in range(rows):
         spread[j * lon : (j + 1) * lon, :] = spread_matrix(where, j, capacity)
@@ -457,23 +474,19 @@
     return jax.ShapeDtypeStruct(dims, dtype)
 
 
-def second_exchange(flag, first, slots, dense, size, links):
-    out = shape((size, dense.shape[1]), BF16)
-
-    def send():
-        rest = pl.pallas_call(
-            functools.partial(rest_kernel, first),
-            out_shape=out,
-            in_specs=[VMEM, VMEM],
-            out_specs=VMEM,
-            name="rest",
-        )(slots, dense)
-        return lax.ppermute(rest, "lat", links)
-
-    def skip():
-        return pl.pallas_call(blank_kernel, out_shape=out, out_specs=ANY, name="blank")()
-
-    return lax.cond(flag, send, skip)
+def send_rest(first, slots, dense, size, links):
+    rest = pl.pallas_call(
+        functools.partial(rest_kernel, first),
+        out_shape=shape((size, dense.shape[1]), BF16),
+        in_specs=[VMEM, VMEM],
+        out_specs=VMEM,
+        name="rest",
+    )(slots, dense)
+    return lax.ppermute(rest, "lat", links)
+
+
+def blank(outs):
+    return pl.pallas_call(blank_kernel, out_shape=outs, out_specs=[ANY] * len(outs), name="blank")()
 
 
 def local(
@@ -498,7 +511,7 @@
     here = lax.axis_index("lat")
     odd = (here % 2).astype(jnp.int32)
     flip = odd.reshape(1)
-    linked = (here > 0) & (here < count - 1)
+    linked = ((here > 0) & (here < count - 1)).astype(jnp.int32).reshape(1)
     pairs = [(i, i ^ 1) for i in range(count)]
     links = [(i, i + 1) for i in range(1, count - 1, 2)]
     links = links + [(b, a) for a, b in links]
@@ -525,99 +538,124 @@
     far = lax.ppermute(sent, "lat", links)
     near = lax.ppermute(own, "lat", pairs)
 
-    own_slots, over = pl.pallas_call(
-        reach_kernel,
-        out_shape=[shape((8, lon), F32)] * 2,
-        in_specs=[SMEM, ANY, VMEM, VMEM],
-        out_specs=[VMEM] * 2,
-        name="reach",
-    )(flip, near, codes, slots)
-    over = jnp.maximum(over, lax.ppermute(over, "lat", links))
-    first_over = linked & (over[0, 0] > 0.0)
-    second_over = linked & (over[0, 1] > 0.0)
-    rest = second_exchange(first_over, FAR_CELLS, slots, own, cells - FAR_CELLS, links)
-
     c_row = courant.reshape(1, levels)
-    slot_ids = jnp.arange(listed, dtype=jnp.int32)
-    observed = slot_ids < obs_count[0]
-    where_at = obs_index[0]
-    where_at = jnp.where(odd == 1, where_at + (rows - 1 - 2 * (where_at // lon)) * lon, where_at)
-    where_at = jnp.where(observed, where_at, -1)
-    quality = jnp.where(observed, obs_quality[0].astype(F32), 0.0)
-
     kept_shape = [shape((2 * lon, levels), F32)] * 3
     slope_shape = shape((listed, hidden_size), F32)
-    slope_one, slope_two, kept_a, kept_b, kept_c, pick, place, place_far, near_codes = pl.pallas_call(
-        near_kernel,
-        out_shape=[slope_shape, slope_shape]
-        + kept_shape
-        + [
-            shape((listed, cells), BF16),
-            shape((cells, listed), BF16),
-            shape((FAR_COLUMNS, listed), BF16),
-            shape((head, lon), F32),
-        ],
-        in_specs=[SMEM, ANY] + [VMEM] * 10,
-        out_specs=[VMEM] * 9,
-        scratch_shapes=[
-            pltpu.VMEM((lon, lon), F32),
-            pltpu.VMEM((6, 2 * lon, 4 * lon), BF16),
-            pltpu.VMEM((2 * cells, levels), BF16),
-            pltpu.VMEM((2, 6 * lon, levels), BF16),
-            pltpu.VMEM((2, 6 * lon, levels), F32),
-            pltpu.VMEM((listed, hidden_size), BF16),
-        ],
-        compiler_params=params(),
-        cost_estimate=pl.CostEstimate(flops=4_000_000_000, bytes_accessed=16_000_000, transcendentals=1_000_000),
-        name="near",
-    )(
-        flip, rest, tangent, codes, near, c_row, background[0], w_first, w_second,
-        where_at.reshape(listed, 1), where_at.reshape(1, listed), own_slots,
-    )
-
-    cells_own, sent, far_codes = pl.pallas_call(
-        observe_kernel,
-        out_shape=[
-            shape((cells, levels), BF16),
-            shape((FAR_COLUMNS, levels), BF16),
-            shape((head, lon), F32),
-        ],
-        in_specs=[SMEM, SMEM, VMEM, VMEM, VMEM, ANY] + [VMEM] * 14,
-        out_specs=[VMEM] * 3,
-        scratch_shapes=[
-            pltpu.VMEM((lon, lon), F32),
-            pltpu.VMEM((8, 2 * lon, 4 * lon), BF16),
-            pltpu.VMEM((6 * lon, levels), BF16),
-            pltpu.VMEM((2, 6 * lon, levels), BF16),
-            pltpu.VMEM((2, 6 * lon, levels), F32),
-            pltpu.VMEM((cells, levels), BF16),
-            pltpu.VMEM((listed, levels), BF16),
-            pltpu.VMEM((listed, levels), BF16),
-            pltpu.VMEM((cells - FAR_CELLS, levels), BF16),
-            pltpu.SemaphoreType.DMA((1,)),
-        ],
-        compiler_params=params(),
-        name="observe",
-    )(
-        flip, first_over.astype(jnp.int32).reshape(1), tangent, codes, far, rest, c_row,
-        slope_one, slope_two, kept_a, kept_b, kept_c, w_first, w_second, w_third,
-        pick, place, place_far, quality.reshape(listed, 1), chan_weight.reshape(1, -1),
-    )
+
+    def run_near():
+        return pl.pallas_call(
+            near_kernel,
+            out_shape=[slope_shape, slope_shape]
+            + kept_shape
+            + [
+                shape((listed, cells), BF16),
+                shape((cells, listed), BF16),
+                shape((FAR_COLUMNS, listed), BF16),
+                shape((head, lon), F32),
+                shape((listed, 1), F32),
+                shape((8, lon), F32),
+            ],
+            in_specs=[SMEM, SMEM] + [VMEM] * 9,
+            out_specs=[VMEM] * 11,
+            scratch_shapes=[
+                pltpu.VMEM((lon, lon), F32),
+                pltpu.VMEM((6, 2 * lon, 4 * lon), BF16),
+                pltpu.VMEM((2 * cells, levels), BF16),
+                pltpu.VMEM((2, 6 * lon, levels), BF16),
+                pltpu.VMEM((2, 6 * lon, levels), F32),
+                pltpu.VMEM((listed, hidden_size), BF16),
+            ],
+            compiler_params=params(),
+            cost_estimate=pl.CostEstimate(flops=4_000_000_000, bytes_accessed=16_000_000, transcendentals=1_000_000),
+            name="near",
+        )(
+            flip, obs_count, tangent, codes, near, c_row, background[0], w_first, w_second, obs_index, obs_quality,
+        )
+
+    column_shape = [shape((cells, levels), BF16), shape((FAR_COLUMNS, levels), BF16)]
+
+    def run_observe(redo, parts, rest):
+        slope_one, slope_two, kept_a, kept_b, kept_c, pick, place, place_far, _, quality, _ = parts
+        rest_specs = [ANY] if redo else []
+        body = functools.partial(observe_kernel, redo)
+        rest_args = [rest] if redo else []
+        rest_scratch = [pltpu.VMEM((cells - FAR_CELLS, levels), BF16), pltpu.SemaphoreType.DMA((1,))]
+
+        def kernel(*refs):
+            refs = list(refs)
+            if not redo:
+                refs.insert(6, None)
+                refs = refs + [None, None]
+            body(*refs)
+
+        return pl.pallas_call(
+            kernel,
+            out_shape=column_shape + [shape((head, lon), F32), shape((1,), jnp.int32)],
+            in_specs=[SMEM, SMEM] + [VMEM] * 4 + rest_specs + [VMEM] * 14,
+            out_specs=[VMEM] * 3 + [SMEM],
+            scratch_shapes=[
+                pltpu.VMEM((lon, lon), F32),
+                pltpu.VMEM((8, 2 * lon, 4 * lon), BF16),
+                pltpu.VMEM((6 * lon, levels), BF16),
+                pltpu.VMEM((2, 6 * lon, levels), BF16),
+                pltpu.VMEM((2, 6 * lon, levels), F32),
+                pltpu.VMEM((cells, levels), BF16),
+                pltpu.VMEM((listed, levels), BF16),
+                pltpu.VMEM((listed, levels), BF16),
+            ]
+            + (rest_scratch if redo else []),
+            compiler_params=params(),
+            name="observe",
+        )(
+            flip, linked, slots, tangent, codes, far, *rest_args, c_row,
+            slope_one, slope_two, kept_a, kept_b, kept_c, w_first, w_second, w_third,
+            pick, place, place_far, quality, chan_weight.reshape(1, -1),
+        )
+
+    parts = run_near()
+    near_codes, own_slots = parts[8], parts[10]
+    cells_own, sent, far_codes, over = run_observe(False, parts, None)
+
+    def observe_again():
+        rest = send_rest(FAR_CELLS, slots, own, cells - FAR_CELLS, links)
+        return run_observe(True, run_near(), rest)[:2]
+
+    redone = lax.cond(over[0] > 0, observe_again, lambda: blank(column_shape))
+    cells_own, sent = pl.pallas_call(
+        choose_kernel,
+        out_shape=column_shape,
+        in_specs=[SMEM] + [ANY] * 4,
+        out_specs=[ANY] * 2,
+        scratch_shapes=[pltpu.SemaphoreType.DMA((2,))],
+        input_output_aliases={1: 0, 2: 1},
+        name="choose",
+    )(over, cells_own, sent, *redone)
 
     columns_far = lax.ppermute(sent, "lat", links)
     cells_near = lax.ppermute(cells_own, "lat", pairs)
 
-    rest = second_exchange(second_over, FAR_COLUMNS, own_slots, cells_own, cells - FAR_COLUMNS, links)
-    kept_a, kept_b, kept_c, mats, spread, far_slots = pl.pallas_call(
+    far_slots, over = pl.pallas_call(
+        reach_kernel,
+        out_shape=[shape((8, lon), F32), shape((1,), jnp.int32)],
+        in_specs=[SMEM, SMEM, VMEM, VMEM],
+        out_specs=[VMEM, SMEM],
+        name="reach",
+    )(flip, linked, own_slots, far_codes)
+    left = cells - FAR_COLUMNS
+    rest = lax.cond(
+        over[0] > 0,
+        lambda: send_rest(FAR_COLUMNS, own_slots, cells_own, left, links),
+        lambda: blank([shape((left, levels), BF16)])[0],
+    )
+    kept_a, kept_b, kept_c, mats, spread = pl.pallas_call(
         near_adjoint_kernel,
         out_shape=kept_shape
         + [
             shape((8, 2 * lon, 4 * lon), BF16),
             shape((cells, FAR_COLUMNS), BF16),
-            shape((8, lon), F32),
         ],
-        in_specs=[SMEM, ANY] + [VMEM] * 6,
-        out_specs=[VMEM] * 6,
+        in_specs=[SMEM, ANY] + [VMEM] * 7,
+        out_specs=[VMEM] * 5,
         scratch_shapes=[
             pltpu.VMEM((lon, lon), F32),
             pltpu.VMEM((6, 2 * lon, 4 * lon), BF16),
@@ -628,7 +666,7 @@
         compiler_params=params(),
         cost_estimate=pl.CostEstimate(flops=2_000_000_000, bytes_accessed=8_000_000, transcendentals=0),
         name="near_adjoint",
-    )(flip, rest, cells_own, cells_near, codes, near_codes, far_codes, c_row)
+    )(flip, rest, cells_own, cells_near, codes, near_codes, far_codes, far_slots, c_row)
 
     return pl.pallas_call(
         far_adjoint_kernel,
@@ -646,7 +684,7 @@
         compiler_params=params(),
         name="far_adjoint",
     )(
-        flip, second_over.astype(jnp.int32).reshape(1), cells_own, columns_far, rest, c_row,
+        flip, over, cells_own, columns_far, rest, c_row,
         kept_a, kept_b, kept_c, mats, spread, far_slots,
     )
 

time: 73.5 us -> 63.9 us (0.87)
  local copies, waits for them, and re-layouts: 9.91 us -> 2.1 us
  other arithmetic: 3.67 us -> 0 us
  Pallas kernels: 33.2 us -> 36.5 us
  starting transfers between devices: 8.27 us -> 5.78 us
  waiting for transfers between devices: 15.5 us -> 16.6 us
    ppermute x1, waiting for transfers between devices: 0.01 us -> 7.44 us  [local(): far = lax.ppermute(sent, 'lat', links)]
    pallas_call x5 -> x6, Pallas kernels: 19.9 us -> 25.7 us  [the longest x1 15.3 us: run_observe(): pl.pallas_call(kernel, out_shape=column_shape + [shape((head, lon), F32),...]
    ppermute x1 -> x0, waiting for transfers between devices: 5.59 us -> none  [local(): over = jnp.maximum(over, lax.ppermute(over, 'lat', links))]
    unnamed x26 -> x18, local copies, waits for them, and re-layouts: 7.58 us -> 2.1 us
    select_n x3 -> x0, other arithmetic: 2.99 us -> none  [the longest x2 1.87 us: local(): where_at = jnp.where(observed, where_at, -1)]
    ppermute x1 -> x0, starting transfers between devices: 2.49 us -> none  [local(): over = jnp.maximum(over, lax.ppermute(over, 'lat', links))]
    pallas_call x1, Pallas kernels: 4.29 us -> 2.76 us  [local(): pl.pallas_call(near_adjoint_kernel, out_shape=kept_shape + [shape((8, 2 *...]
    pallas_call x1, Pallas kernels: 5.91 us -> 5.04 us  [local(): pl.pallas_call(far_adjoint_kernel, out_shape=shape((rows, lon, levels), F...]
  transfers between devices with their start and end apart: 5 -> 4, of which waited for: 3 -> 2; matrix products, arithmetic and copies ran while one was open for 8% -> 0% of each run, Pallas kernels for 14% -> 20%
where the time goes in v3:
time: 63.9 us; the launch traced here: 63.5 us
  Pallas kernels  36.5 us (57%)
  waiting for transfers between devices  16.6 us (26%)
  starting transfers between devices  5.78 us (9%)
  between operations  2.28 us (4%)
  local copies, waits for them, and re-layouts  2.1 us (3%)
    pallas_call x1, Pallas kernels, run_observe(): pl.pallas_call(kernel, out_shape=column_shape + [shape((head, lon), F32),...  15.3 us
    ppermute x1, waiting for transfers between devices, local(): columns_far = lax.ppermute(sent, 'lat', links)  9.19 us
    pallas_call x1, Pallas kernels, run_near(): pl.pallas_call(near_kernel, out_shape=[slope_shape, slope_shape] + kept_s...  7.91 us
    ppermute x1, waiting for transfers between devices, local(): far = lax.ppermute(sent, 'lat', links)  7.44 us
    pallas_call x1, Pallas kernels, local(): pl.pallas_call(far_adjoint_kernel, out_shape=shape((rows, lon, levels), F...  5.04 us
    ppermute x1, starting transfers between devices, local(): far = lax.ppermute(sent, 'lat', links)  3.05 us
    pallas_call x1, Pallas kernels, local(): pl.pallas_call(pack_kernel, out_shape=[shape((cells + head, levels), BF16...  3 us
    pallas_call x1, Pallas kernels, local(): pl.pallas_call(near_adjoint_kernel, out_shape=kept_shape + [shape((8, 2 *...  2.76 us
  transfers between devices with their start and end apart: 4, of which 2 were waited for; matrix products, arithmetic and copies ran while one was open for 0% of the time, Pallas kernels for 20%

profile of v3, /device:TPU:25, one launch (start us, length us, event | category | flops | bytes accessed | tf_op | source)
XLA Modules:
  0.0 63.5 jit_solution(4417996205405121174)
XLA Ops:
  0.0 0.0 copy-start.8
  0.0 0.0 copy-start.7
  0.0 0.0 copy-start.6
  0.0 0.0 copy-start.4
  0.0 3.0 %pack.1 = (bf16[528,1024]{1,0:T(8,128)(2,1)S(1)}, bf16[320,1024]{1,0:T(8,128)(2,1)}, f32[16,128]{1,0:T(8,128)S(1)}, f32[8,128]{1,0:T(8,128)S(1)}) custom-call(s32[1]{0:T(128)} %bitcast.2.flip.refs_0_, f32[4,128,1024]{2,1,0:T(8,128)} %refs_3_.1, s32[4,4,128]{2,1,0:T(4,128)} %wind.1), custom_call_target="tpu_custom_call" | custom-call | tf_op jit(solution)/shard_map/pack/pallas_call | solution.py:519
  3.0 0.7 %collective-permute-start.2 = (bf16[528,1024]{1,0:T(8,128)(2,1)S(1)}, bf16[528,1024]{1,0:T(8,128)(2,1)}, u32[]{:S(2)}, u32[]{:S(2)}) collective-permute-start(bf16[528,1024]{1,0:T(8,128)(2,1)S(1)} %get-tuple-element.107), channel_id=1, source_target_pairs={{0,1},{1,0},{2,3},{3,2},{4,5},{5,4},{6,7},{7,6},{8,9},{9,8},{10,11... | collective-permute-start | bytes 3244040 | tf_op jit(solution)/shard_map/ppermute | solution.py:539
  3.8 3.0 %collective-permute-start.3 = (bf16[320,1024]{1,0:T(8,128)(2,1)}, bf16[320,1024]{1,0:T(8,128)(2,1)S(1)}, u32[]{:S(2)}, u32[]{:S(2)}) collective-permute-start(bf16[320,1024]{1,0:T(8,128)(2,1)} %get-tuple-element.110), channel_id=1, source_target_pairs={{1,2},{3,4},{5,6},{7,8},{9,10},{11,12},{13,14},{2,1},{4,3},{6,5},{... | collective-permute-start | bytes 1966088 | tf_op jit(solution)/shard_map/ppermute | solution.py:538
  7.5 0.0 collective-permute-done.2.near
  7.5 0.0 copy-done.8
  7.5 0.0 copy-done.7
  7.5 0.0 copy-done.6
  7.5 0.0 copy-done.4
  7.5 0.0 copy-start.5
  7.6 7.9 %near.3 = (f32[480,1024]{1,0:T(8,128)S(1)}, f32[480,1024]{1,0:T(8,128)S(1)}, f32[256,1024]{1,0:T(8,128)S(1)}, f32[256,1024]{1,0:T(8,128)S(1)}, f32[256,1024]{1,0...) custom-call(s32[1]{0:T(128)} %bitcast.2.flip.refs_0_, ...), custom_call_target="tpu_custom_call" | custom-call | flops 4000000000 | bytes 16000000 | tf_op jit(solution)/shard_map/near/pallas_call | solution.py:546
  15.5 7.4 %collective-permute-done.3.refs_5_ = bf16[320,1024]{1,0:T(8,128)(2,1)S(1)} collective-permute-done((bf16[320,1024]{1,0:T(8,128)(2,1)}, bf16[320,1024]{1,0:T(8,128)(2,1)S(1)}, u32[]{:S(2)}, u32[]{:S(2)}) %collective-permute-start.3) | collective-permute-done | bytes 655392 | tf_op jit(solution)/shard_map/ppermute | solution.py:538
  22.9 0.0 copy-done.5
  22.9 15.3 %observe.3 = (bf16[512,1024]{1,0:T(8,128)(2,1)S(1)}, bf16[272,1024]{1,0:T(8,128)(2,1)S(1)}, f32[16,128]{1,0:T(8,128)S(1)}, s32[1]{0:T(128)}) custom-call(s32[1]{0:T(128)} %bitcast.2.flip.refs_0_, s32[1]{0:T(128)} %bitcast.3.refs_1_.linked, f32[8,128]{1,0:T(8,128)S(1)} %get-tuple-element.109.refs_2_, f32[4,128,1024]{2,1,0:T(8,128)} %refs_3_.1, ...), custom_call_target="tpu_custom_call" | custom-call | tf_op jit(solution)/shard_map/observe/pallas_call | solution.py:591
  38.3 0.0 copy-start
  38.3 0.8 %copy-done = bf16[272,1024]{1,0:T(8,128)(2,1)} copy-done((bf16[272,1024]{1,0:T(8,128)(2,1)}, bf16[272,1024]{1,0:T(8,128)(2,1)S(1)}, u32[]{:S(2)}) %copy-start) | copy-done | bytes 557080
  39.1 0.0 copy-start.1
  39.1 0.6 copy-done.1
  40.3 0.2 conditional.2
  40.5 0.0 copy-start.2
  40.6 0.7 %choose.1 = (bf16[512,1024]{1,0:T(8,128)(2,1)S(1)}, bf16[272,1024]{1,0:T(8,128)(2,1)}) custom-call(s32[1]{0:T(128)} %get-tuple-element.122.flag, bf16[512,1024]{1,0:T(8,128)(2,1)S(1)} %get-tuple-element.123._one, bf16[272,1024]{1,0:T(8,128)(2,1)} %copy-done, ...), custom_call_target="tpu_custom_call", output_to_operand_aliasing={{0}: (1, {}), {1}: (2, {})} | custom-call | tf_op jit(solution)/shard_map/choose/pallas_call | solution.py:624
  41.2 0.1 collective-permute-start.5
  41.3 1.9 %collective-permute-start.4 = (bf16[272,1024]{1,0:T(8,128)(2,1)}, bf16[272,1024]{1,0:T(8,128)(2,1)S(1)}, u32[]{:S(2)}, u32[]{:S(2)}) collective-permute-start(bf16[272,1024]{1,0:T(8,128)(2,1)} %get-tuple-element.128), channel_id=1, source_target_pairs={{1,2},{3,4},{5,6},{7,8},{9,10},{11,12},{13,14},{2,1},{4,3},{6,5},{... | collective-permute-start | bytes 1671176 | tf_op jit(solution)/shard_map/ppermute | solution.py:634
  43.2 1.8 %reach.1 = (f32[8,128]{1,0:T(8,128)}, s32[1]{0:T(128)}) custom-call(s32[1]{0:T(128)} %bitcast.2.flip.refs_0_, s32[1]{0:T(128)} %bitcast.3.refs_1_.linked, f32[8,128]{1,0:T(8,128)S(1)} %get-tuple-element.108.own_slots, f32[16,128]{1,0:T(8,128)} %copy-done.1), custom_call_target="tpu_custom_call" | custom-call | tf_op jit(solution)/shard_map/reach/pallas_call | solution.py:637
  45.7 0.0 collective-permute-done.5.cells_near
  45.7 0.0 copy-done.2
  45.7 0.0 copy-start.3
  45.7 0.7 %copy-done.3 = f32[8,128]{1,0:T(8,128)S(1)} copy-done((f32[8,128]{1,0:T(8,128)S(1)}, f32[8,128]{1,0:T(8,128)}, u32[]{:S(2)}) %copy-start.3) | copy-done | bytes 4120
  46.4 2.8 %near_adjoint.1 = (f32[256,1024]{1,0:T(8,128)S(1)}, f32[256,1024]{1,0:T(8,128)S(1)}, f32[256,1024]{1,0:T(8,128)S(1)}, bf16[8,256,512]{2,1,0:T(8,128)(2,1)S(1)}, bf16[512,272]{1,0:T(8,128)(2,1)S(1)}) custom-call(s32[1]{0:T(128)} %bitcast.2.flip.refs_0_, bf16[240,1024]{1,0:T(8,128)(2,1)} %get-tuple-element.141.rest, ...), custom_call_target="tpu_custom_call" | custom-call | flops 2000000000 | bytes 8000000 | tf_op jit(solution)/shard_map/near_adjoint/pallas_call | solution.py:650
  49.1 9.2 %collective-permute-done.4.far = bf16[272,1024]{1,0:T(8,128)(2,1)S(1)} collective-permute-done((bf16[272,1024]{1,0:T(8,128)(2,1)}, bf16[272,1024]{1,0:T(8,128)(2,1)S(1)}, u32[]{:S(2)}, u32[]{:S(2)}) %collective-permute-start.4) | collective-permute-done | bytes 557088 | tf_op jit(solution)/shard_map/ppermute | solution.py:634
  58.3 5.0 %far_adjoint.1 = f32[4,128,1024]{2,1,0:T(8,128)} custom-call(s32[1]{0:T(128)} %bitcast.2.flip.refs_0_, s32[1]{0:T(128)} %get-tuple-element.121.flag, bf16[512,1024]{1,0:T(8,128)(2,1)S(1)} %get-tuple-element.127.cells_own, bf16[272,1024]{1,0:T(8,128)(2,1)S(1)} %collective-permute-done.4.far, bf16[240,1024]{1,0:T(8,128)(2,1)} %get-tuple-element.141.rest, ...), custom_call_target="tpu_custom_call" | custom-call | tf_op jit(solution)/shard_map/far_adjoint/pallas_call | solution.py:671
  (3 shorter events, 0.0 us)
Async XLA Ops:
  0.0 7.5 %copy-start.8 = (bf16[1,480]{1,0:T(2,128)(2,1)S(1)}, bf16[1,480]{1,0:T(2,128)(2,1)}, u32[]{:S(2)}) copy-start(bf16[1,480]{1,0:T(2,128)(2,1)} %obs_quality.1) | copy-start | bytes 2884
  0.0 7.5 %copy-start.7 = (s32[1,480]{1,0:T(1,128)S(1)}, s32[1,480]{1,0:T(1,128)}, u32[]{:S(2)}) copy-start(s32[1,480]{1,0:T(1,128)} %obs_index.1) | copy-start | bytes 5764
  0.0 7.5 %copy-start.6 = (bf16[1,480,1024]{2,1,0:T(8,128)(2,1)S(1)}, bf16[1,480,1024]{2,1,0:T(8,128)(2,1)}, u32[]{:S(2)}) copy-start(bf16[1,480,1024]{2,1,0:T(8,128)(2,1)} %param.21) | copy-start | bytes 2949124
  0.0 7.5 %copy-start.4 = (f32[1024]{0:T(1024)S(1)}, f32[1024]{0:T(1024)}, u32[]{:S(2)}) copy-start(f32[1024]{0:T(1024)} %param.17) | copy-start | bytes 12292
  3.0 4.5 %collective-permute-start.2 = (bf16[528,1024]{1,0:T(8,128)(2,1)S(1)}, bf16[528,1024]{1,0:T(8,128)(2,1)}, u32[]{:S(2)}, u32[]{:S(2)}) collective-permute-start(bf16[528,1024]{1,0:T(8,128)(2,1)S(1)} %get-tuple-element.107), channel_id=1, source_target_pairs={{0,1},{1,0},{2,3},{3,2},{4,5},{5,4},{6,7},{7,6},{8,9},{9,8},{10,11... | collective-permute-start | bytes 3244040 | tf_op jit(solution)/shard_map/ppermute | solution.py:539
  3.8 19.1 %collective-permute-start.3 = (bf16[320,1024]{1,0:T(8,128)(2,1)}, bf16[320,1024]{1,0:T(8,128)(2,1)S(1)}, u32[]{:S(2)}, u32[]{:S(2)}) collective-permute-start(bf16[320,1024]{1,0:T(8,128)(2,1)} %get-tuple-element.110), channel_id=1, source_target_pairs={{1,2},{3,4},{5,6},{7,8},{9,10},{11,12},{13,14},{2,1},{4,3},{6,5},{... | collective-permute-start | bytes 1966088 | tf_op jit(solution)/shard_map/ppermute | solution.py:538
  7.5 15.4 %copy-start.5 = (f32[1024]{0:T(1024)S(1)}, f32[1024]{0:T(1024)}, u32[]{:S(2)}) copy-start(f32[1024]{0:T(1024)} %param.25) | copy-start | bytes 12292
  38.3 0.8 %copy-start = (bf16[272,1024]{1,0:T(8,128)(2,1)}, bf16[272,1024]{1,0:T(8,128)(2,1)S(1)}, u32[]{:S(2)}) copy-start(bf16[272,1024]{1,0:T(8,128)(2,1)S(1)} %get-tuple-element.124._two) | copy-start | bytes 1671172
  39.1 0.6 copy-start.1
  40.5 5.1 %copy-start.2 = (f32[16,128]{1,0:T(8,128)S(1)}, f32[16,128]{1,0:T(8,128)}, u32[]{:S(2)}) copy-start(f32[16,128]{1,0:T(8,128)} %copy-done.1) | copy-start | bytes 24580
  41.2 4.5 %collective-permute-start.5 = (bf16[512,1024]{1,0:T(8,128)(2,1)S(1)}, bf16[512,1024]{1,0:T(8,128)(2,1)S(1)}, u32[]{:S(2)}, u32[]{:S(2)}) collective-permute-start(bf16[512,1024]{1,0:T(8,128)(2,1)S(1)} %get-tuple-element.127.cells_own), channel_id=1, source_target_pairs={{0,1},{1,0},{2,3},{3,2},{4,5},{5,4},{6,7},{7,6},{8,9},{9,8},{10,11... | collective-permute-start | bytes 3145736 | tf_op jit(solution)/shard_map/ppermute | solution.py:635
  41.3 17.0 %collective-permute-start.4 = (bf16[272,1024]{1,0:T(8,128)(2,1)}, bf16[272,1024]{1,0:T(8,128)(2,1)S(1)}, u32[]{:S(2)}, u32[]{:S(2)}) collective-permute-start(bf16[272,1024]{1,0:T(8,128)(2,1)} %get-tuple-element.128), channel_id=1, source_target_pairs={{1,2},{3,4},{5,6},{7,8},{9,10},{11,12},{13,14},{2,1},{4,3},{6,5},{... | collective-permute-start | bytes 1671176 | tf_op jit(solution)/shard_map/ppermute | solution.py:634
  45.7 0.7 %copy-start.3 = (f32[8,128]{1,0:T(8,128)S(1)}, f32[8,128]{1,0:T(8,128)}, u32[]{:S(2)}) copy-start(f32[8,128]{1,0:T(8,128)} %get-tuple-element.130.far_slots) | copy-start | bytes 12292
